TPU v7x, 32 devices: a whole 2x2x4 slice. The times are simulated.
32 devices in a mesh: row: 4 (over y, x), col: 8 (over z, core).
Axes of the slice: x: 2, y: 2, z: 4, core: 2. Of those that a mesh axis runs over, the one named last changes fastest.
Arguments:
- a_tiles: bfloat16 [256, 16, 128, 128], P(('row', 'col')), may hold values from -0.5 to 0.5
- a_cols: int32 [256, 16], P(('row', 'col')), may hold values from -1 to 31, as said below
- p_tiles: bfloat16 [256, 2, 128, 128], P(('row', 'col')), may hold values from -0.375 to 0.375
- p_cols: int32 [256, 2], P(('row', 'col')), may hold values from 0 to 3, all different within a row
- send_list: int32 [32, 24], P(('row', 'col')), may hold values from 0 to 7
Outputs:
- coarse: float32 [2048, 1536], P(('row', 'col'))
Inputs may be any that keep to these rules, and one draw needn't show every extreme that they name: a_cols is -1 for an empty slot, else an index below 32 into the buffer of step one; slot 0 of every block row is live and names the row itself; rows of the first row group never use t = 0 and rows of the last never t = 2; a device holds at most 80 live slots, and some device exactly 80. The 2 entries of a row of p_cols differ.
All inputs are finite; a program needn't handle non-finite values.
Results may differ from a plain program's by a relative error of at most 0.0029.
Values may be sent and summed in bfloat16 or wider, within the bound.
A program may use at most 64 MiB of HBM per device.

v0:
```python
import jax
import jax.numpy as jnp
from jax import lax
from jax.sharding import PartitionSpec as P

CG = 4


def from_behind(value, axis, steps):
    count = lax.axis_size(axis)
    leading, last = (max(0, -steps), min(count, count - steps))
    return lax.ppermute(value, axis, [(source, source + steps) for source in range(leading, last)])


def exchange_rows(send_tiles, send_cols):
    return (
        lax.all_to_all(send_tiles, "col", split_axis=0, concat_axis=0, tiled=True),
        lax.all_to_all(send_cols, "col", split_axis=0, concat_axis=0, tiled=True),
    )


def body(a_tiles, a_cols, p_tiles, p_cols, send_list):
    col_count = lax.axis_size("col")
    own_rows, slot_count = a_cols.shape
    tile_count = p_cols.shape[1]
    block_size = a_tiles.shape[-1]
    window = 3 * CG
    stream_ids = jnp.arange(3, dtype=jnp.int32)
    picked = send_list[0]
    send_tiles = p_tiles[picked].reshape(col_count, 3, tile_count, block_size, block_size)
    send_cols = p_cols[picked].reshape(col_count, 3, tile_count)
    got_tiles, got_cols = exchange_rows(send_tiles, send_cols)
    lower_tiles, lower_cols = from_behind((got_tiles[:, 0], got_cols[:, 0]), "row", 1)
    upper_tiles, upper_cols = from_behind((got_tiles[:, 2], got_cols[:, 2]), "row", -1)
    ghost_tiles = jnp.stack([lower_tiles, got_tiles[:, 1], upper_tiles], axis=1)
    ghost_cols = jnp.stack([lower_cols, got_cols[:, 1], upper_cols], axis=1)
    buffer_tiles = jnp.concatenate(
        [p_tiles, ghost_tiles.reshape(3 * col_count, tile_count, block_size, block_size)], axis=0
    )
    buffer_cols = jnp.concatenate(
        [
            p_cols + CG,
            (ghost_cols + CG * stream_ids[None, :, None]).reshape(3 * col_count, tile_count),
        ],
        axis=0,
    )
    flat_tiles = a_tiles.reshape(own_rows * slot_count, block_size, block_size)
    flat_cols = a_cols.reshape(-1)
    slot_pos = jnp.arange(own_rows * slot_count, dtype=jnp.int32)

    def add_block(coarse_acc, slot_ids):
        col_ids = flat_cols[slot_ids]
        is_live = (col_ids >= 0).astype(jnp.float32)
        buffer_index = jnp.maximum(col_ids, 0)
        a_block = flat_tiles[slot_ids]
        p_block = buffer_tiles[buffer_index]
        tile_prod = jnp.einsum(
            "kxy,kpyz->kpxz", a_block, p_block, preferred_element_type=jnp.float32
        )
        tile_prod = tile_prod * is_live[:, None, None, None]
        target = (slot_ids // slot_count)[:, None] * window + buffer_cols[buffer_index]
        coarse_acc = coarse_acc.at[target.reshape(-1)].add(
            tile_prod.reshape(-1, block_size, block_size)
        )
        return (coarse_acc, None)

    start_acc = jnp.zeros((own_rows * window, block_size, block_size), jnp.float32)
    accumulated, unused = lax.scan(add_block, start_acc, slot_pos.reshape(-1, slot_count))
    product_rows = accumulated.reshape(own_rows, window, block_size, block_size).transpose(
        0, 2, 1, 3
    )
    product_rows = product_rows.reshape(own_rows * block_size, window * block_size).astype(
        jnp.bfloat16
    )
    member = (p_cols[:, :, None] == jnp.arange(CG, dtype=jnp.int32)).astype(jnp.bfloat16)
    dense_prolong = jnp.einsum(
        "fpm,fpxy->fxmy", member, p_tiles, preferred_element_type=jnp.float32
    )
    dense_prolong = dense_prolong.astype(jnp.bfloat16).reshape(
        own_rows * block_size, CG * block_size
    )
    return lax.psum_scatter(
        jnp.dot(dense_prolong.T, product_rows, preferred_element_type=jnp.float32),
        "col",
        scatter_dimension=0,
        tiled=True,
    )


def solution(mesh):
    in_specs = (
        P(("row", "col"), None, None, None),
        P(("row", "col"), None),
        P(("row", "col"), None, None, None),
        P(("row", "col"), None),
        P(("row", "col"), None),
    )
    out_specs = P(("row", "col"), None)
    return jax.shard_map(body, mesh=mesh, in_specs=in_specs, out_specs=out_specs, check_vma=False)
```

profile of v0, /device:TPU:0, one launch (start us, length us, event | category | flops | bytes accessed | tf_op | source)
XLA Modules:
  0.0 287.9 jit_solution(1581057987729568662)
XLA Ops:
  6.5 0.7 fusion.14
  7.2 3.0 %gather_fusion.5 = bf16[24,2,128,128]{3,2,1,0:T(8,128)(2,1)} fusion(bf16[8,2,128,128]{3,2,1,0:T(8,128)(2,1)} %param.9, s32[1024]{0:T(1024)S(1)} %pad_clamp_fusion.2), kind=kCustom, calls=%fused_computation.5 | custom fusion | bytes 3145824 | tf_op jit(solution)/shard_map/gather | solution.py:30
  10.2 6.5 %all-to-all-start.1 = ((bf16[8,3,2,128,128]{4,3,2,1,0:T(8,128)(2,1)}), bf16[8,3,2,128,128]{4,3,2,1,0:T(8,128)(2,1)S(1)}, u32[]{:S(2)}, u32[]{:S(2)}) async-start(bf16[8,3,2,128,128]{4,3,2,1,0:T(8,128)(2,1)} %bitcast.86), calls=%async_computation.1 | async-start | bytes 3145728 | tf_op jit(solution)/shard_map/all_to_all | solution.py:17
  18.3 2.0 convolution_convert_fusion
  20.3 34.2 %all-to-all-done.1 = bf16[8,3,2,128,128]{4,3,2,1,0:T(8,128)(2,1)S(1)} async-done(((bf16[8,3,2,128,128]{4,3,2,1,0:T(8,128)(2,1)}), bf16[8,3,2,128,128]{4,3,2,1,0:T(8,128)(2,1)S(1)}, u32[]{:S(2)}, u32[]{:S(2)}) %all-to-all-start.1) | async-done | bytes 1572896 | tf_op jit(solution)/shard_map/all_to_all | solution.py:17
  54.5 3.3 %all-to-all-start = ((s32[8,3,2]{1,2,0:T(2,128)}), s32[8,3,2]{1,2,0:T(2,128)S(1)}, u32[]{:S(2)}, u32[]{:S(2)}) async-start(s32[8,3,2]{1,2,0:T(2,128)} %copy.67), calls=%async_computation | async-start | bytes 16384 | tf_op jit(solution)/shard_map/all_to_all | solution.py:18
  57.9 0.9 slice_bitcast_fusion.1
  58.8 3.4 %collective-permute-start.2 = (bf16[8,2,128,128]{3,2,1,0:T(8,128)(2,1)}, bf16[8,2,128,128]{3,2,1,0:T(8,128)(2,1)S(1)}, u32[]{:S(2)}, u32[]{:S(2)}) collective-permute-start(bf16[8,2,128,128]{3,2,1,0:T(8,128)(2,1)} %get-tuple-element.145), channel_id=1, source_target_pairs={{0,8},{8,16},{16,24},{1,9},{9,17},{17,25},{2,10},{10,18},{18,26},{... | collective-permute-start | bytes 1572872 | tf_op jit(solution)/shard_map/ppermute | solution.py:12
  62.3 1.3 collective-permute-start.3
  63.7 4.5 %collective-permute-start = (s32[8,2]{0,1:T(2,128)S(1)}, s32[8,2]{0,1:T(2,128)S(1)}, u32[]{:S(2)}, u32[]{:S(2)}) collective-permute-start(s32[8,2]{0,1:T(2,128)S(1)} %bitcast.92), channel_id=1, source_target_pairs={{0,8},{8,16},{16,24},{1,9},{9,17},{17,25},{2,10},{10,18},{18,26},{... | collective-permute-start | bytes 200 | tf_op jit(solution)/shard_map/ppermute | solution.py:12
  68.4 1.3 collective-permute-start.1
  69.8 4.5 %collective-permute-done = s32[8,2]{0,1:T(2,128)S(1)} collective-permute-done((s32[8,2]{0,1:T(2,128)S(1)}, s32[8,2]{0,1:T(2,128)S(1)}, u32[]{:S(2)}, u32[]{:S(2)}) %collective-permute-start) | collective-permute-done | bytes 96 | tf_op jit(solution)/shard_map/ppermute | solution.py:12
  74.2 13.1 %collective-permute-done.1 = s32[8,2]{0,1:T(2,128)S(1)} collective-permute-done((s32[8,2]{0,1:T(2,128)S(1)}, s32[8,2]{0,1:T(2,128)S(1)}, u32[]{:S(2)}, u32[]{:S(2)}) %collective-permute-start.1) | collective-permute-done | bytes 96 | tf_op jit(solution)/shard_map/ppermute | solution.py:12
  87.9 1.5 pad_maximum_fusion
  89.4 3.4 %broadcast_in_dim.2 = f32[96,128,128]{2,1,0:T(8,128)} broadcast(f32[]{:T(128)} %constant.68.clone.1), dimensions={} | broadcast | bytes 6291460 | tf_op jit(solution)/shard_map/broadcast_in_dim | solution.py:67
  92.9 134.4 %while.12 = (s32[]{:T(128)}, f32[96,128,128]{2,1,0:T(8,128)}, s32[8,16]{1,0:T(8,128)S(1)}, s32[128]{0:T(128)S(1)}, s32[32,2]{1,0:T(8,128)S(1)}, /*index=5*/bf16[...) while((s32[]{:T(128)}, f32[96,128,128]{2,1,0:T(8,128)}, s32[8,16]{1,0:T(8,128)S(1)}, ...), condition=%wide.region_2.3_spmd, body=%wide.region_0.2_spmd.sunk | while | flops 135268832 | bytes 17312092 | solution.py:68
  93.6 2.3 gather_fusion.2
  95.9 2.8 gather_fusion.3
  98.8 1.9 convolution_multiply_fusion.2
  100.7 1.9 copy.95
  103.3 6.4 %scatter_fusion = f32[96,128,128]{2,1,0:T(8,128)} fusion(f32[96,128,128]{2,1,0:T(8,128)} %get-tuple-element.203, s32[32]{0:T(128)S(1)} %fusion.26, f32[32,128,128]{2,1,0:T(8,128)S(1)} %copy.95), kind=kCustom, calls=%fused_computation.6.clone.1 | custom fusion | flops 524288 | bytes 6291584 | tf_op jit(solution)/shard_map/while/body/eval_jaxpr/scatter-add | solution.py:62
  110.5 2.3 gather_fusion.2
  112.8 2.8 gather_fusion.3
  115.7 1.9 convolution_multiply_fusion.2
  117.5 1.9 copy.95
  120.2 6.3 %scatter_fusion = f32[96,128,128]{2,1,0:T(8,128)} fusion(f32[96,128,128]{2,1,0:T(8,128)} %get-tuple-element.203, s32[32]{0:T(128)S(1)} %fusion.26, f32[32,128,128]{2,1,0:T(8,128)S(1)} %copy.95), kind=kCustom, calls=%fused_computation.6.clone.1 | custom fusion | flops 524288 | bytes 6291584 | tf_op jit(solution)/shard_map/while/body/eval_jaxpr/scatter-add | solution.py:62
  126.5 0.7 gather_fusion
  127.2 2.3 gather_fusion.2
  129.6 2.8 gather_fusion.3
  132.4 1.9 convolution_multiply_fusion.2
  134.3 1.9 copy.95
  137.0 6.5 %scatter_fusion = f32[96,128,128]{2,1,0:T(8,128)} fusion(f32[96,128,128]{2,1,0:T(8,128)} %get-tuple-element.203, s32[32]{0:T(128)S(1)} %fusion.26, f32[32,128,128]{2,1,0:T(8,128)S(1)} %copy.95), kind=kCustom, calls=%fused_computation.6.clone.1 | custom fusion | flops 524288 | bytes 6291584 | tf_op jit(solution)/shard_map/while/body/eval_jaxpr/scatter-add | solution.py:62
  143.5 0.7 gather_fusion
  144.2 2.3 gather_fusion.2
  146.5 2.8 gather_fusion.3
  149.4 1.9 convolution_multiply_fusion.2
  151.3 1.9 copy.95
  154.0 6.1 %scatter_fusion = f32[96,128,128]{2,1,0:T(8,128)} fusion(f32[96,128,128]{2,1,0:T(8,128)} %get-tuple-element.203, s32[32]{0:T(128)S(1)} %fusion.26, f32[32,128,128]{2,1,0:T(8,128)S(1)} %copy.95), kind=kCustom, calls=%fused_computation.6.clone.1 | custom fusion | flops 524288 | bytes 6291584 | tf_op jit(solution)/shard_map/while/body/eval_jaxpr/scatter-add | solution.py:62
  160.1 0.7 gather_fusion
  160.8 2.3 gather_fusion.2
  163.1 2.8 gather_fusion.3
  166.0 1.9 convolution_multiply_fusion.2
  167.8 1.9 copy.95
  170.5 6.3 %scatter_fusion = f32[96,128,128]{2,1,0:T(8,128)} fusion(f32[96,128,128]{2,1,0:T(8,128)} %get-tuple-element.203, s32[32]{0:T(128)S(1)} %fusion.26, f32[32,128,128]{2,1,0:T(8,128)S(1)} %copy.95), kind=kCustom, calls=%fused_computation.6.clone.1 | custom fusion | flops 524288 | bytes 6291584 | tf_op jit(solution)/shard_map/while/body/eval_jaxpr/scatter-add | solution.py:62
  177.5 2.3 gather_fusion.2
  179.9 2.8 gather_fusion.3
  182.8 1.9 convolution_multiply_fusion.2
  184.6 1.9 copy.95
  187.3 6.4 %scatter_fusion = f32[96,128,128]{2,1,0:T(8,128)} fusion(f32[96,128,128]{2,1,0:T(8,128)} %get-tuple-element.203, s32[32]{0:T(128)S(1)} %fusion.26, f32[32,128,128]{2,1,0:T(8,128)S(1)} %copy.95), kind=kCustom, calls=%fused_computation.6.clone.1 | custom fusion | flops 524288 | bytes 6291584 | tf_op jit(solution)/shard_map/while/body/eval_jaxpr/scatter-add | solution.py:62
  193.7 0.7 gather_fusion
  194.4 2.3 gather_fusion.2
  196.7 2.8 gather_fusion.3
  199.6 1.9 convolution_multiply_fusion.2
  201.5 1.9 copy.95
  204.2 6.5 %scatter_fusion = f32[96,128,128]{2,1,0:T(8,128)} fusion(f32[96,128,128]{2,1,0:T(8,128)} %get-tuple-element.203, s32[32]{0:T(128)S(1)} %fusion.26, f32[32,128,128]{2,1,0:T(8,128)S(1)} %copy.95), kind=kCustom, calls=%fused_computation.6.clone.1 | custom fusion | flops 524288 | bytes 6291584 | tf_op jit(solution)/shard_map/while/body/eval_jaxpr/scatter-add | solution.py:62
  211.4 2.3 gather_fusion.2
  213.8 2.8 gather_fusion.3
  216.6 1.9 convolution_multiply_fusion.2
  218.5 1.9 copy.95
  221.2 6.1 %scatter_fusion = f32[96,128,128]{2,1,0:T(8,128)} fusion(f32[96,128,128]{2,1,0:T(8,128)} %get-tuple-element.203, s32[32]{0:T(128)S(1)} %fusion.26, f32[32,128,128]{2,1,0:T(8,128)S(1)} %copy.95), kind=kCustom, calls=%fused_computation.6.clone.1 | custom fusion | flops 524288 | bytes 6291584 | tf_op jit(solution)/shard_map/while/body/eval_jaxpr/scatter-add | solution.py:62
  227.3 3.5 %convert_element_type.31 = bf16[96,128,128]{2,1,0:T(8,128)(2,1)S(1)} convert(f32[96,128,128]{2,1,0:T(8,128)} %get-tuple-element.95) | non-fusion elementwise | flops 1572864 | bytes 9437184 | tf_op jit(solution)/shard_map/convert_element_type | solution.py:72
  230.7 3.1 %copy.75 = bf16[8,12,128,128]{2,0,3,1:T(8,128)(2,1)} copy(bf16[8,12,128,128]{3,2,1,0:T(8,128)(2,1)S(1)} %bitcast.85) | data formatting | bytes 6291456 | tf_op jit(solution)/shard_map/convert_element_type | solution.py:72
  233.9 5.7 %fusion.4 = f32[512,1536]{1,0:T(8,128)} fusion(bf16[192,8,8,128]{3,2,1,0:T(8,128)(2,1)} %bitcast.88, bf16[128,8,4,128]{3,2,1,0:T(4,128)(2,1)} %bitcast.96), kind=kOutput, calls=%fused_computation.25 | convolution fusion | flops 1610612736 | bytes 7340032 | tf_op jit(solution)/shard_map/dot_general | solution.py:83
  239.6 41.4 %reduce-scatter.2.cloned.1.call-done = f32[64,1536]{1,0:T(8,128)} async-done(((f32[512,1536]{1,0:T(8,128)}), f32[64,1536]{1,0:T(8,128)}) %reduce-scatter.2.cloned.1.call-update) | async-done | bytes 393232 | tf_op jit(solution)/shard_map/reduce_scatter | solution.py:82
  (118 shorter events, 11.4 us)
Async XLA Ops:
  10.2 6.5 %copy-start.1 = (s32[8,2]{0,1:T(2,128)S(1)}, s32[8,2]{0,1:T(2,128)}, u32[]{:S(2)}) copy-start(s32[8,2]{0,1:T(2,128)} %param.10) | copy-start | bytes 196
  10.2 8.0 %copy-start.2 = (s32[8,16]{1,0:T(8,128)S(1)}, s32[8,16]{1,0:T(8,128)}, u32[]{:S(2)}) copy-start(s32[8,16]{1,0:T(8,128)} %param.8) | copy-start | bytes 1540
  10.2 8.1 %copy-start = (bf16[8,2,128,128]{3,2,1,0:T(8,128)(2,1)S(1)}, bf16[8,2,128,128]{3,2,1,0:T(8,128)(2,1)}, u32[]{:S(2)}) copy-start(bf16[8,2,128,128]{3,2,1,0:T(8,128)(2,1)} %param.9) | copy-start | bytes 1572868
  10.2 44.3 %all-to-all-start.1 = ((bf16[8,3,2,128,128]{4,3,2,1,0:T(8,128)(2,1)}), bf16[8,3,2,128,128]{4,3,2,1,0:T(8,128)(2,1)S(1)}, u32[]{:S(2)}, u32[]{:S(2)}) async-start(bf16[8,3,2,128,128]{4,3,2,1,0:T(8,128)(2,1)} %bitcast.86), calls=%async_computation.1 | async-start | bytes 3145728 | tf_op jit(solution)/shard_map/all_to_all | solution.py:17
  54.5 9.1 %all-to-all-start = ((s32[8,3,2]{1,2,0:T(2,128)}), s32[8,3,2]{1,2,0:T(2,128)S(1)}, u32[]{:S(2)}, u32[]{:S(2)}) async-start(s32[8,3,2]{1,2,0:T(2,128)} %copy.67), calls=%async_computation | async-start | bytes 16384 | tf_op jit(solution)/shard_map/all_to_all | solution.py:18
  57.8 223.2 %reduce-scatter.2.cloned.1.call-start = ((), (), s32[]{:S(2)}) async-start(), calls=%async_computation.3 | async-start | bytes 3538944 | tf_op jit(solution)/shard_map/reduce_scatter | solution.py:82
  58.8 28.9 %collective-permute-start.2 = (bf16[8,2,128,128]{3,2,1,0:T(8,128)(2,1)}, bf16[8,2,128,128]{3,2,1,0:T(8,128)(2,1)S(1)}, u32[]{:S(2)}, u32[]{:S(2)}) collective-permute-start(bf16[8,2,128,128]{3,2,1,0:T(8,128)(2,1)} %get-tuple-element.145), channel_id=1, source_target_pairs={{0,8},{8,16},{16,24},{1,9},{9,17},{17,25},{2,10},{10,18},{18,26},{... | collective-permute-start | bytes 1572872 | tf_op jit(solution)/shard_map/ppermute | solution.py:12
  62.3 25.5 %collective-permute-start.3 = (bf16[8,2,128,128]{3,2,1,0:T(8,128)(2,1)S(1)}, bf16[8,2,128,128]{3,2,1,0:T(8,128)(2,1)S(1)}, u32[]{:S(2)}, u32[]{:S(2)}) collective-permute-start(bf16[8,2,128,128]{3,2,1,0:T(8,128)(2,1)S(1)} %get-tuple-element.147), channel_id=1, source_target_pairs={{8,0},{16,8},{24,16},{9,1},{17,9},{25,17},{10,2},{18,10},{26,18},{... | collective-permute-start | bytes 1572872 | tf_op jit(solution)/shard_map/ppermute | solution.py:12
  63.7 10.5 %collective-permute-start = (s32[8,2]{0,1:T(2,128)S(1)}, s32[8,2]{0,1:T(2,128)S(1)}, u32[]{:S(2)}, u32[]{:S(2)}) collective-permute-start(s32[8,2]{0,1:T(2,128)S(1)} %bitcast.92), channel_id=1, source_target_pairs={{0,8},{8,16},{16,24},{1,9},{9,17},{17,25},{2,10},{10,18},{18,26},{... | collective-permute-start | bytes 200 | tf_op jit(solution)/shard_map/ppermute | solution.py:12
  68.4 19.0 %collective-permute-start.1 = (s32[8,2]{0,1:T(2,128)S(1)}, s32[8,2]{0,1:T(2,128)S(1)}, u32[]{:S(2)}, u32[]{:S(2)}) collective-permute-start(s32[8,2]{0,1:T(2,128)S(1)} %bitcast.93), channel_id=1, source_target_pairs={{8,0},{16,8},{24,16},{9,1},{17,9},{25,17},{10,2},{18,10},{26,18},{... | collective-permute-start | bytes 200 | tf_op jit(solution)/shard_map/ppermute | solution.py:12
Sparse Core Ops, SparseCore 0:
  239.7 41.2 reduce-scatter.1
where the time goes:
time: 290 us; the launch traced here: 288 us
  waiting for transfers between devices  93.3 us (32%)
  local copies, waits for them, and re-layouts  79.9 us (28%)
  other arithmetic  57.6 us (20%)
  matrix products  22.7 us (8%)
  starting transfers between devices  20.4 us (7%)
  between operations  13.5 us (5%)
    scatter-add x8, other arithmetic, add_block(): coarse_acc.at[target.reshape(-1)]  50.7 us
    reduce_scatter x1, waiting for transfers between devices, body(): lax.psum_scatter(jnp.dot(dense_prolong.T, product_rows, preferred_element...  41.4 us
    all_to_all x1, waiting for transfers between devices, exchange_rows(): lax.all_to_all(send_tiles, 'col', split_axis=0, concat_axis=0, tiled=True)  34.2 us
    gather x8, local copies, waits for them, and re-layouts, add_block(): a_block = flat_tiles[slot_ids]  22.7 us
    gather x8, local copies, waits for them, and re-layouts, add_block(): p_block = buffer_tiles[buffer_index]  18.7 us
    ppermute x4, waiting for transfers between devices, from_behind(): lax.ppermute(value, axis, [(source, source + steps) for source in range(l...  17.6 us
    reshape x8, local copies, waits for them, and re-layouts, add_block(): tile_prod.reshape(-1, block_size, block_size)  15.3 us
    dot_general x8, matrix products, add_block(): jnp.einsum('kxy,kpyz->kpxz', a_block, p_block, preferred_element_type=jnp...  15 us
  transfers between devices with their start and end apart: 7, of which 4 were waited for; matrix products, arithmetic and copies ran while one was open for 2% of the time, Pallas kernels for 0%

commit v1 on v0

v1 whole, which is shorter than its diff:
```python
import functools

import jax
import jax.numpy as jnp
from jax import lax
from jax.experimental import pallas as pl
from jax.experimental.pallas import tpu as pltpu
from jax.sharding import PartitionSpec as P

CG = 4
MESH = pl.DeviceIdType.MESH
UNROLL = 4
VMEM_LIMIT = 48 * 1024 * 1024


def far_first(index, count, step):
    half = count // 2
    side, local = index // half, index % half
    other = step < half
    side = jnp.where(other, 1 - side, side)
    return side * half + (local + step) % half


def exchange_kernel(
    row_count, col_count, p_ref, pc_ref, sl_ref, buf_ref, cols_ref,
    send, send_cols, tile_ss, tile_rs, cols_ss, cols_rs,
):
    g, c = lax.axis_index("row"), lax.axis_index("col")
    own = p_ref.shape[0]
    bs = p_ref.shape[-1]

    def group_ok(group):
        return (group >= 0) & (group < row_count)

    barrier = pltpu.get_barrier_semaphore()

    @pl.loop(0, col_count)
    def _(other):
        for t in range(3):
            group = g + 1 - t

            @pl.when(group_ok(group) & ((other != c) | (t != 1)))
            def _():
                pl.semaphore_signal(barrier, inc=1, device_id=(group, other), device_id_type=MESH)

    lane = lax.broadcasted_iota(jnp.int32, (1, bs), 1)

    @pl.loop(0, col_count)
    def _(other):
        for t in range(3):
            j = other * 3 + t
            r = sl_ref[0, j]
            send[j, :, 0:bs] = p_ref[r, 0]
            send[j, :, bs : 2 * bs] = p_ref[r, 1]
            send_cols[j] = jnp.where(lane == 0, pc_ref[r, 0], pc_ref[r, 1]) + t * CG

    peers = col_count - 1
    peers = peers + jnp.where(g > 0, col_count, 0) + jnp.where(g < row_count - 1, col_count, 0)
    pl.semaphore_wait(barrier, peers)

    def tiles_copy(source, target, group, other):
        return pltpu.make_async_remote_copy(
            src_ref=send.at[source], dst_ref=buf_ref.at[own + target],
            send_sem=tile_ss.at[source], recv_sem=tile_rs.at[target],
            device_id=(group, other), device_id_type=MESH,
        )

    def cols_copy(source, target, group, other):
        return pltpu.make_async_remote_copy(
            src_ref=send_cols.at[source], dst_ref=cols_ref.at[own + target],
            send_sem=cols_ss.at[source], recv_sem=cols_rs.at[target],
            device_id=(group, other), device_id_type=MESH,
        )

    @pl.loop(0, col_count)
    def _(step):
        other = far_first(c, col_count, step)
        for t in range(3):
            group = g + 1 - t

            @pl.when(group_ok(group) & ((other != c) | (t != 1)))
            def _():
                tiles_copy(other * 3 + t, c * 3 + t, group, other).start()
                cols_copy(other * 3 + t, c * 3 + t, group, other).start()

    @pl.loop(0, own)
    def _(r):
        buf_ref[r, :, 0:bs] = p_ref[r, 0]
        buf_ref[r, :, bs : 2 * bs] = p_ref[r, 1]
        cols_ref[r] = jnp.where(lane == 0, pc_ref[r, 0], pc_ref[r, 1]) + CG

    mine = c * 3 + 1
    buf_ref[own + mine] = send[mine]
    cols_ref[own + mine] = send_cols[mine]

    @pl.loop(0, col_count)
    def _(other):
        for t in range(3):
            slot = other * 3 + t
            not_self = (other != c) | (t != 1)

            @pl.when(group_ok(g + 1 - t) & not_self)
            def _():
                tiles_copy(slot, slot, g + 1 - t, other).wait_send()
                cols_copy(slot, slot, g + 1 - t, other).wait_send()

            @pl.when(group_ok(g + t - 1) & not_self)
            def _():
                tiles_copy(slot, slot, g + t - 1, other).wait_recv()
                cols_copy(slot, slot, g + t - 1, other).wait_recv()


def product_kernel(
    col_count, acols_ref, pc_ref, cols_ref, a_ref, p_ref, buf_ref, prod_ref, dpt_ref,
    acc, slot_of, src_of, to_first, to_second,
):
    rows, slots = acols_ref.shape
    bs = a_ref.shape[-1]
    window = 3 * CG
    dump = rows * window

    def collect(s, count):
        i = s // slots
        b = acols_ref[i, s % slots]
        src = jnp.maximum(b, 0)
        slot_of[count] = s
        src_of[count] = src
        to_first[count] = i * window + cols_ref[src, 0, 0]
        to_second[count] = i * window + cols_ref[src, 0, 1]
        return count + (b >= 0).astype(jnp.int32)

    live = lax.fori_loop(0, rows * slots, collect, jnp.int32(0))
    for extra in range(UNROLL):
        slot_of[live + extra] = 0
        src_of[live + extra] = 0
        to_first[live + extra] = dump
        to_second[live + extra] = dump

    @pl.loop(0, rows)
    def _(i):
        acc[pl.ds(i * window, window)] = jnp.zeros((window, bs, bs), jnp.float32)

    dpt_ref[...] = jnp.zeros_like(dpt_ref)
    owners = col_count // CG
    piece = bs // owners
    half = CG * bs // 2
    for i in range(rows):
        for p in range(p_ref.shape[1]):
            flipped = p_ref[i, p].astype(jnp.float32).T.astype(jnp.bfloat16)
            m = pc_ref[i, p]
            for u in range(owners):
                start = (u % 2) * half + (m * (owners // 2) + u // 2) * piece
                dpt_ref[pl.ds(pl.multiple_of(start, piece), piece), i * bs : (i + 1) * bs] = (
                    flipped[u * piece : (u + 1) * piece]
                )

    @pl.loop(0, (live + UNROLL - 1) // UNROLL)
    def _(step):
        first = step * UNROLL
        outs = [
            jnp.dot(a_ref[slot_of[first + u]], buf_ref[src_of[first + u]], preferred_element_type=jnp.float32)
            for u in range(UNROLL)
        ]
        for u in range(UNROLL):
            acc[to_first[first + u]] += outs[u][:, :bs]
            acc[to_second[first + u]] += outs[u][:, bs:]

    @pl.loop(0, rows)
    def _(i):
        for l in range(window):
            prod_ref[pl.ds(pl.multiple_of(i * bs, bs), bs), l * bs : (l + 1) * bs] = acc[
                i * window + l
            ].astype(jnp.bfloat16)


def reduce_kernel(
    col_count, dpt_ref, prod_ref, out_ref, pair_send, pair_recv, kept, line_send, line_recv,
    pair_ss, pair_rs, line_ss, line_rs,
):
    g, c = lax.axis_index("row"), lax.axis_index("col")
    chips = col_count // 2
    z, k = c // 2, c % 2
    piece, width = out_ref.shape
    half = chips * piece
    chunk = 512

    barrier = pltpu.get_barrier_semaphore()
    pl.semaphore_signal(barrier, inc=1, device_id=(g, 2 * z + 1 - k), device_id_type=MESH)

    @pl.loop(1, chips)
    def _(step):
        other = (z + step) % chips
        pl.semaphore_signal(barrier, inc=1, device_id=(g, 2 * other + k), device_id_type=MESH)

    def multiply(core, target):
        rows = dpt_ref[pl.ds(pl.multiple_of(core * half, half), half), :]
        for n in range(0, width, chunk):
            part = jnp.dot(rows, prod_ref[:, n : n + chunk], preferred_element_type=jnp.float32)
            for s in range(chips):
                target[s, :, n : n + chunk] = part[s * piece : (s + 1) * piece]

    multiply(1 - k, pair_send)
    pl.semaphore_wait(barrier, chips)

    def pair_copy(s):
        return pltpu.make_async_remote_copy(
            src_ref=pair_send.at[s], dst_ref=pair_recv.at[s],
            send_sem=pair_ss.at[s], recv_sem=pair_rs.at[s],
            device_id=(g, 2 * z + 1 - k), device_id_type=MESH,
        )

    def line_copy(source, target, other):
        return pltpu.make_async_remote_copy(
            src_ref=line_send.at[source], dst_ref=line_recv.at[target],
            send_sem=line_ss.at[source], recv_sem=line_rs.at[target],
            device_id=(g, 2 * other + k), device_id_type=MESH,
        )

    @pl.loop(0, chips)
    def _(step):
        pair_copy(far_first(z, chips, step)).start()

    multiply(k, kept)

    @pl.loop(0, chips)
    def _(step):
        other = far_first(z, chips, step)
        pair_copy(other).wait_recv()

        @pl.when(other != z)
        def _():
            line_send[other] = (kept[other] + pair_recv[other]).astype(jnp.bfloat16)
            line_copy(other, z, other).start()

        @pl.when(other == z)
        def _():
            out_ref[...] = kept[other] + pair_recv[other]

    @pl.loop(1, chips)
    def _(step):
        other = (z + step) % chips
        line_copy(other, other, other).wait_recv()
        out_ref[...] += line_recv[other].astype(jnp.float32)
        line_copy(other, other, other).wait_send()

    @pl.loop(0, chips)
    def _(s):
        pair_copy(s).wait_send()


def body(row_count, col_count, a_tiles, a_cols, p_tiles, p_cols, send_list):
    own, slots = a_cols.shape
    tiles = p_cols.shape[1]
    bs = a_tiles.shape[-1]
    ghosts = 3 * col_count
    window = 3 * CG
    vmem = pl.BlockSpec(memory_space=pltpu.VMEM)
    smem = pl.BlockSpec(memory_space=pltpu.SMEM)
    dma = pltpu.SemaphoreType.DMA
    buffer_tiles, buffer_cols = pl.pallas_call(
        functools.partial(exchange_kernel, row_count, col_count),
        out_shape=(
            jax.ShapeDtypeStruct((own + ghosts, bs, tiles * bs), jnp.bfloat16),
            jax.ShapeDtypeStruct((own + ghosts, 1, bs), jnp.int32),
        ),
        in_specs=[vmem, smem, smem],
        out_specs=(vmem, vmem),
        scratch_shapes=[
            pltpu.VMEM((ghosts, bs, tiles * bs), jnp.bfloat16),
            pltpu.VMEM((ghosts, 1, bs), jnp.int32),
            dma((ghosts,)), dma((ghosts,)), dma((ghosts,)), dma((ghosts,)),
        ],
        compiler_params=pltpu.CompilerParams(
            collective_id=0, has_side_effects=True, vmem_limit_bytes=VMEM_LIMIT
        ),
        name="exchange",
    )(p_tiles, p_cols, send_list)
    room = own * slots + UNROLL
    product_rows, prolong_t = pl.pallas_call(
        functools.partial(product_kernel, col_count),
        out_shape=(
            jax.ShapeDtypeStruct((own * bs, window * bs), jnp.bfloat16),
            jax.ShapeDtypeStruct((CG * bs, own * bs), jnp.bfloat16),
        ),
        in_specs=[smem, smem, smem, vmem, vmem, vmem],
        out_specs=(vmem, vmem),
        scratch_shapes=[pltpu.VMEM((own * window + 1, bs, bs), jnp.float32)]
        + [pltpu.SMEM((room,), jnp.int32)] * 4,
        compiler_params=pltpu.CompilerParams(vmem_limit_bytes=VMEM_LIMIT),
        name="product",
    )(
        a_cols, p_cols, buffer_cols[:, :, :tiles],
        a_tiles.reshape(own * slots, bs, bs), p_tiles, buffer_tiles,
    )
    chips = col_count // 2
    piece = CG * bs // col_count
    blocks = (chips, piece, window * bs)
    return pl.pallas_call(
        functools.partial(reduce_kernel, col_count),
        out_shape=jax.ShapeDtypeStruct((piece, window * bs), jnp.float32),
        in_specs=[vmem, vmem],
        out_specs=vmem,
        scratch_shapes=[
            pltpu.VMEM(blocks, jnp.float32),
            pltpu.VMEM(blocks, jnp.float32),
            pltpu.VMEM(blocks, jnp.float32),
            pltpu.VMEM(blocks, jnp.bfloat16),
            pltpu.VMEM(blocks, jnp.bfloat16),
            dma((chips,)), dma((chips,)), dma((chips,)), dma((chips,)),
        ],
        compiler_params=pltpu.CompilerParams(
            collective_id=1, has_side_effects=True, vmem_limit_bytes=VMEM_LIMIT
        ),
        name="reduce",
    )(prolong_t, product_rows)


def solution(mesh):
    in_specs = (
        P(("row", "col"), None, None, None),
        P(("row", "col"), None),
        P(("row", "col"), None, None, None),
        P(("row", "col"), None),
        P(("row", "col"), None),
    )
    out_specs = P(("row", "col"), None)
    return jax.shard_map(
        functools.partial(body, mesh.shape["row"], mesh.shape["col"]),
        mesh=mesh, in_specs=in_specs, out_specs=out_specs, check_vma=False,
    )
```

time: 290 us -> 82.5 us (0.28)
  the two profiles are of different devices: /device:TPU:0 before, /device:TPU:9 now
where the time goes in v1:
time: 82.5 us; the launch traced here: 82.1 us
  Pallas kernels  76.3 us (92%)
  local copies, waits for them, and re-layouts  5.77 us (7%)
    pallas_call x1, Pallas kernels, body(): pl.pallas_call(functools.partial(exchange_kernel, row_count, col_count),...  41.7 us
    pallas_call x1, Pallas kernels, body(): pl.pallas_call(functools.partial(reduce_kernel, col_count), out_shape=jax...  24.1 us
    pallas_call x1, Pallas kernels, body(): pl.pallas_call(functools.partial(product_kernel, col_count), out_shape=(j...  10.5 us
    unnamed x10, local copies, waits for them, and re-layouts  5.77 us

profile of v1, /device:TPU:9, one launch (start us, length us, event | category | flops | bytes accessed | tf_op | source)
XLA Modules:
  0.0 82.1 jit_solution(14231562798414002844)
XLA Ops:
  0.0 0.8 copy.7.pc_ref
  0.8 0.0 copy-start.1
  0.8 1.0 %copy-done.1 = bf16[8,2,128,128]{3,2,1,0:T(8,128)(2,1)S(1)} copy-done((bf16[8,2,128,128]{3,2,1,0:T(8,128)(2,1)S(1)}, bf16[8,2,128,128]{3,2,1,0:T(8,128)(2,1)}, u32[]{:S(2)}) %copy-start.1) | copy-done | bytes 524312
  1.8 0.0 copy-start.3
  1.8 0.7 copy-done.3
  2.5 41.7 %exchange.1 = (bf16[32,128,256]{2,1,0:T(8,128)(2,1)S(1)}, s32[32,1,128]{2,1,0:T(1,128)S(1)}) custom-call(bf16[8,2,128,128]{3,2,1,0:T(8,128)(2,1)S(1)} %copy-done.1, s32[8,2]{1,0:T(8,128)S(1)} %copy.7.pc_ref, s32[1,24]{1,0:T(1,128)S(1)} %copy-done.3), custom_call_target="tpu_custom_call" | custom-call | tf_op jit(solution)/shard_map/exchange/pallas_call | solution.py:260
  44.2 0.0 copy-start.2
  44.2 0.7 copy-done.2
  44.9 10.5 %product.1 = (bf16[1024,1536]{1,0:T(8,128)(2,1)}, bf16[512,1024]{1,0:T(8,128)(2,1)S(1)}) custom-call(s32[8,16]{1,0:T(8,128)S(1)} %copy-done.2, s32[8,2]{1,0:T(8,128)S(1)} %copy.7.pc_ref, s32[32,1,2]{2,1,0:T(1,128)S(1)} %bitcast.2, bf16[128,128,128]{2,1,0:T(8,128)(2,1)} %bitcast.3, bf16[8,2,128,128]{3,2,1,0:T(8,128)(2,1)S(1)} %copy-done.1, ...), custom_call_target="tpu_custom_call" | custom-call | tf_op jit(solution)/shard_map/product/pallas_call | solution.py:279
  55.3 0.0 copy-start
  55.4 1.9 %copy-done = bf16[1024,1536]{1,0:T(8,128)(2,1)S(1)} copy-done((bf16[1024,1536]{1,0:T(8,128)(2,1)S(1)}, bf16[1024,1536]{1,0:T(8,128)(2,1)}, u32[]{:S(2)}) %copy-start) | copy-done | bytes 3145752
  57.2 24.1 %reduce.1 = f32[64,1536]{1,0:T(8,128)S(1)} custom-call(bf16[512,1024]{1,0:T(8,128)(2,1)S(1)} %get-tuple-element.11.dpt_ref, bf16[1024,1536]{1,0:T(8,128)(2,1)S(1)} %copy-done), custom_call_target="tpu_custom_call" | custom-call | tf_op jit(solution)/shard_map/reduce/pallas_call | solution.py:298
  81.3 0.7 copy.9
Async XLA Ops:
  0.8 1.0 %copy-start.1 = (bf16[8,2,128,128]{3,2,1,0:T(8,128)(2,1)S(1)}, bf16[8,2,128,128]{3,2,1,0:T(8,128)(2,1)}, u32[]{:S(2)}) copy-start(bf16[8,2,128,128]{3,2,1,0:T(8,128)(2,1)} %p_ref.3) | copy-start | bytes 1572868
  1.8 0.7 copy-start.3
  44.2 0.7 copy-start.2
  55.3 1.9 %copy-start = (bf16[1024,1536]{1,0:T(8,128)(2,1)S(1)}, bf16[1024,1536]{1,0:T(8,128)(2,1)}, u32[]{:S(2)}) copy-start(bf16[1024,1536]{1,0:T(8,128)(2,1)} %get-tuple-element.12.prod_ref) | copy-start | bytes 9437188

commit v2 on v0

v2 whole, which is shorter than its diff:
```python
import functools

import jax
import jax.numpy as jnp
from jax import lax
from jax.experimental import pallas as pl
from jax.experimental.pallas import tpu as pltpu
from jax.sharding import PartitionSpec as P

CG = 4
MESH = pl.DeviceIdType.MESH
ORDER = (1, 0, 2)
VMEM_LIMIT = 56 * 1024 * 1024


def far_first(index, count, step):
    half = count // 2
    side, local = index // half, index % half
    side = jnp.where(step < half, 1 - side, side)
    return side * half + (local + step) % half


def kernel(
    row_count, col_count, a_hbm, p_ref, ac_ref, pc_ref, sl_ref, out_ref,
    a_vm, send, send_cols, recv, recv_cols, dense, rt, prod,
    pair_send, pair_recv, kept, line_send, line_recv,
    a_sem, tile_ss, tile_rs, cols_ss, cols_rs, pair_ss, pair_rs, line_ss, line_rs,
):
    g, c = lax.axis_index("row"), lax.axis_index("col")
    chips = col_count // 2
    z, k = c // 2, c % 2
    own, slots = ac_ref.shape
    bs = p_ref.shape[-1]
    ghosts = 3 * col_count
    zero_row = own + ghosts
    wide = CG * bs
    piece = wide // col_count
    half = wide // 2
    f32, bf16 = jnp.float32, jnp.bfloat16

    def group_ok(group):
        return (group >= 0) & (group < row_count)

    def a_copy(s):
        return pltpu.make_async_copy(
            a_hbm.at[:, s], a_vm.at[:, :, pl.ds(s * bs, bs)], a_sem.at[s]
        )

    barrier = pltpu.get_barrier_semaphore()

    @pl.loop(0, col_count)
    def _(other):
        for t in range(3):
            group = g + 1 - t

            @pl.when(group_ok(group) & ((other != c) | (t != 1)))
            def _():
                pl.semaphore_signal(barrier, inc=1, device_id=(group, other), device_id_type=MESH)

    for s in range(slots):
        a_copy(s).start()

    def pattern(r):
        lane = lax.broadcasted_iota(jnp.int32, (1, 2 * bs), 1)
        return jnp.where(lane < bs, pc_ref[r, 0], pc_ref[r, 1])

    @pl.loop(0, col_count)
    def _(other):
        for t in range(3):
            j = other * 3 + t
            r = sl_ref[0, j]
            send[j, 0] = p_ref[r, 0]
            send[j, 1] = p_ref[r, 1]
            send_cols[j] = pattern(r)

    peers = col_count - 1
    peers = peers + jnp.where(g > 0, col_count, 0) + jnp.where(g < row_count - 1, col_count, 0)
    pl.semaphore_wait(barrier, peers)

    def tiles_copy(source, target, group, other):
        return pltpu.make_async_remote_copy(
            src_ref=send.at[source], dst_ref=recv.at[target],
            send_sem=tile_ss.at[source], recv_sem=tile_rs.at[target],
            device_id=(group, other), device_id_type=MESH,
        )

    def cols_copy(source, target, group, other):
        return pltpu.make_async_remote_copy(
            src_ref=send_cols.at[source], dst_ref=recv_cols.at[target],
            send_sem=cols_ss.at[source], recv_sem=cols_rs.at[target],
            device_id=(group, other), device_id_type=MESH,
        )

    def pair_copy(w):
        return pltpu.make_async_remote_copy(
            src_ref=pair_send.at[w], dst_ref=pair_recv.at[w],
            send_sem=pair_ss.at[w], recv_sem=pair_rs.at[w],
            device_id=(g, 2 * z + 1 - k), device_id_type=MESH,
        )

    def line_copy(w, source, target, other):
        return pltpu.make_async_remote_copy(
            src_ref=line_send.at[w, source], dst_ref=line_recv.at[w, target],
            send_sem=line_ss.at[w, source], recv_sem=line_rs.at[w, target],
            device_id=(g, 2 * other + k), device_id_type=MESH,
        )

    for t in ORDER:
        group = g + 1 - t

        @pl.loop(0, col_count)
        def _(step):
            other = far_first(c, col_count, step)

            @pl.when(group_ok(group) & ((other != c) | (t != 1)))
            def _():
                cols_copy(other * 3 + t, c * 3 + t, group, other).start()
                tiles_copy(other * 3 + t, c * 3 + t, group, other).start()

    def spread(target, tiles, cols):
        first, second = tiles[0].astype(f32), tiles[1].astype(f32)
        for m in range(CG):
            in_first = jnp.where(cols[:, :bs] == m, 1.0, 0.0)
            in_second = jnp.where(cols[:, bs:] == m, 1.0, 0.0)
            dense[target, :, m * bs : (m + 1) * bs] = (
                first * in_first + second * in_second
            ).astype(bf16)

    dense[zero_row] = jnp.zeros((bs, wide), bf16)
    owners = col_count // CG

    @pl.loop(0, own)
    def _(r):
        spread(r, p_ref.at[r], pattern(r))
        first = p_ref[r, 0].astype(f32).T
        second = p_ref[r, 1].astype(f32).T
        for m in range(CG):
            in_first = jnp.where(pc_ref[r, 0] == m, 1.0, 0.0)
            in_second = jnp.where(pc_ref[r, 1] == m, 1.0, 0.0)
            block = (first * in_first + second * in_second).astype(bf16)
            for u in range(owners):
                start = (u % 2) * half + (m * (owners // 2) + u // 2) * piece
                rt[start : start + piece, pl.ds(pl.multiple_of(r * bs, bs), bs)] = block[
                    u * piece : (u + 1) * piece
                ]

    def take_stream(t):
        @pl.loop(0, col_count)
        def _(other):
            slot = other * 3 + t

            @pl.when(group_ok(g + t - 1) & ((other != c) | (t != 1)))
            def _():
                cols_copy(slot, slot, g + t - 1, other).wait_recv()
                tiles_copy(slot, slot, g + t - 1, other).wait_recv()
                spread(own + slot, recv.at[slot], recv_cols[slot])

            if t == 1:

                @pl.when(other == c)
                def _():
                    spread(own + slot, send.at[slot], send_cols[slot])

    def products(w):
        @pl.loop(0, own)
        def _(i):
            index = []
            for s in range(slots):
                b = ac_ref[i, s]
                ghost = jnp.maximum(b - own, 0)
                stream = jnp.where(b < own, 1, ghost % 3)
                index.append(jnp.where((b >= 0) & (stream == w), b, zero_row))
            for n in range(0, wide, 2 * bs):
                total = jnp.zeros((bs, 2 * bs), f32)
                for s in range(0, slots, 2):
                    right = jnp.concatenate(
                        [dense[index[s], :, n : n + 2 * bs], dense[index[s + 1], :, n : n + 2 * bs]],
                        axis=0,
                    )
                    left = a_vm[i, :, s * bs : (s + 2) * bs]
                    total = total + jnp.dot(left, right, preferred_element_type=f32)
                prod[pl.ds(pl.multiple_of(i * bs, bs), bs), n : n + 2 * bs] = total.astype(bf16)

    def restrict(core):
        rows = rt[pl.ds(pl.multiple_of(core * half, half), half), :]
        return jnp.dot(rows, prod[...], preferred_element_type=f32)

    def line_stage(w):
        pair_copy(w).wait_recv()
        columns = slice(w * wide, (w + 1) * wide)

        @pl.loop(0, chips)
        def _(step):
            other = far_first(z, chips, step)
            rows = pl.ds(pl.multiple_of(other * piece, piece), piece)

            @pl.when(other != z)
            def _():
                line_send[w, other] = (kept[w, rows] + pair_recv[w, rows]).astype(bf16)
                line_copy(w, other, z, other).start()

            @pl.when(other == z)
            def _():
                out_ref[:, columns] = kept[w, rows] + pair_recv[w, rows]

    for s in range(slots):
        a_copy(s).wait()
    for n, w in enumerate(ORDER):
        take_stream(w)
        if n == 2:
            line_stage(ORDER[0])
            line_stage(ORDER[1])
        products(w)
        pair_send[w] = restrict(1 - k)
        pair_copy(w).start()
        kept[w] = restrict(k)
    line_stage(ORDER[2])

    for w in ORDER:
        columns = slice(w * wide, (w + 1) * wide)

        @pl.loop(1, chips)
        def _(step):
            other = (z + step) % chips
            line_copy(w, other, other, other).wait_recv()
            out_ref[:, columns] += line_recv[w, other].astype(f32)
            line_copy(w, other, other, other).wait_send()

        pair_copy(w).wait_send()

        @pl.loop(0, col_count)
        def _(other):
            slot = other * 3 + w

            @pl.when(group_ok(g + 1 - w) & ((other != c) | (w != 1)))
            def _():
                cols_copy(slot, slot, g + 1 - w, other).wait_send()
                tiles_copy(slot, slot, g + 1 - w, other).wait_send()


def body(row_count, col_count, a_tiles, a_cols, p_tiles, p_cols, send_list):
    own, slots = a_cols.shape
    tiles = p_cols.shape[1]
    bs = a_tiles.shape[-1]
    ghosts = 3 * col_count
    chips = col_count // 2
    wide = CG * bs
    piece = wide // col_count
    vmem = pl.BlockSpec(memory_space=pltpu.VMEM)
    smem = pl.BlockSpec(memory_space=pltpu.SMEM)
    dma = pltpu.SemaphoreType.DMA
    f32, bf16 = jnp.float32, jnp.bfloat16
    return pl.pallas_call(
        functools.partial(kernel, row_count, col_count),
        out_shape=jax.ShapeDtypeStruct((piece, 3 * wide), f32),
        in_specs=[pl.BlockSpec(memory_space=pl.ANY), vmem, smem, smem, smem],
        out_specs=vmem,
        scratch_shapes=[
            pltpu.VMEM((own, bs, slots * bs), bf16),
            pltpu.VMEM((ghosts, tiles, bs, bs), bf16),
            pltpu.VMEM((ghosts, 1, tiles * bs), jnp.int32),
            pltpu.VMEM((ghosts, tiles, bs, bs), bf16),
            pltpu.VMEM((ghosts, 1, tiles * bs), jnp.int32),
            pltpu.VMEM((own + ghosts + 1, bs, wide), bf16),
            pltpu.VMEM((wide, own * bs), bf16),
            pltpu.VMEM((own * bs, wide), bf16),
            pltpu.VMEM((3, wide // 2, wide), f32),
            pltpu.VMEM((3, wide // 2, wide), f32),
            pltpu.VMEM((3, wide // 2, wide), f32),
            pltpu.VMEM((3, chips, piece, wide), bf16),
            pltpu.VMEM((3, chips, piece, wide), bf16),
            dma((slots,)),
            dma((ghosts,)), dma((ghosts,)), dma((ghosts,)), dma((ghosts,)),
            dma((3,)), dma((3,)), dma((3, chips)), dma((3, chips)),
        ],
        compiler_params=pltpu.CompilerParams(
            collective_id=0, has_side_effects=True, vmem_limit_bytes=VMEM_LIMIT
        ),
        name="triple_product",
    )(a_tiles, p_tiles, a_cols, p_cols, send_list)


def solution(mesh):
    in_specs = (
        P(("row", "col"), None, None, None),
        P(("row", "col"), None),
        P(("row", "col"), None, None, None),
        P(("row", "col"), None),
        P(("row", "col"), None),
    )
    out_specs = P(("row", "col"), None)
    return jax.shard_map(
        functools.partial(body, mesh.shape["row"], mesh.shape["col"]),
        mesh=mesh, in_specs=in_specs, out_specs=out_specs, check_vma=False,
    )
```

time: 290 us -> 65.9 us (0.23)
  waiting for transfers between devices: 93.3 us -> 0 us
  local copies, waits for them, and re-layouts: 79.9 us -> 3.11 us
  Pallas kernels: 0 us -> 62.6 us
  other arithmetic: 57.6 us -> 0 us
  matrix products: 22.7 us -> 0 us
  starting transfers between devices: 20.4 us -> 0 us
  between operations: 13.5 us -> 0.01 us
    pallas_call x0 -> x1, Pallas kernels: none -> 62.6 us  [body(): pl.pallas_call(functools.partial(kernel, row_count, col_count), out_shape...]
    gather x35 -> x0, local copies, waits for them, and re-layouts: 54.8 us -> none  [the longest x8 22.7 us: add_block(): a_block = flat_tiles[slot_ids]]
    scatter-add x8 -> x0, other arithmetic: 50.7 us -> none  [add_block(): coarse_acc.at[target.reshape(-1)]]
    reduce_scatter x1 -> x0, waiting for transfers between devices: 41.4 us -> none  [body(): lax.psum_scatter(jnp.dot(dense_prolong.T, product_rows, preferred_element...]
    all_to_all x2 -> x0, waiting for transfers between devices: 34.2 us -> none  [the longest x1 34.2 us: exchange_rows(): lax.all_to_all(send_tiles, 'col', split_axis=0, concat_axis=0, tiled=True)]
    dot_general x10 -> x0, matrix products: 22.7 us -> none  [the longest x8 15 us: add_block(): jnp.einsum('kxy,kpyz->kpxz', a_block, p_block, preferred_element_type=jnp...]
    ppermute x4 -> x0, waiting for transfers between devices: 17.6 us -> none  [from_behind(): lax.ppermute(value, axis, [(source, source + steps) for source in range(l...]
    reshape x11 -> x0, local copies, waits for them, and re-layouts: 16.1 us -> none  [the longest x8 15.3 us: add_block(): tile_prod.reshape(-1, block_size, block_size)]
  transfers between devices with their start and end apart: 7 -> 0, of which waited for: 4 -> 0; matrix products, arithmetic and copies ran while one was open for 2% -> 0% of each run, Pallas kernels for 0% -> 0%
where the time goes in v2:
time: 65.9 us; the launch traced here: 65.7 us
  Pallas kernels  62.6 us (95%)
  local copies, waits for them, and re-layouts  3.11 us (5%)
    pallas_call x1, Pallas kernels, body(): pl.pallas_call(functools.partial(kernel, row_count, col_count), out_shape...  62.6 us
    unnamed x2, local copies, waits for them, and re-layouts  3.11 us

profile of v2, /device:TPU:0, one launch (start us, length us, event | category | flops | bytes accessed | tf_op | source)
XLA Modules:
  0.0 65.7 jit_solution(17360150224067506039)
XLA Ops:
  0.0 1.3 %copy.6.pc_ref = s32[8,2]{1,0:T(8,128)} copy(s32[8,2]{0,1:T(2,128)} %param.8) | data formatting | bytes 128 | tf_op args[3]
  1.3 62.6 %triple_product.1 = f32[64,1536]{1,0:T(8,128)} custom-call(bf16[8,16,128,128]{3,2,1,0:T(8,128)(2,1)} %a_hbm.1, bf16[8,2,128,128]{3,2,1,0:T(8,128)(2,1)} %p_ref.1, s32[8,16]{1,0:T(8,128)} %ac_ref.1, s32[8,2]{1,0:T(8,128)} %copy.6.pc_ref, s32[1,24]{1,0:T(1,128)} %sl_ref.1), custom_call_target="tpu_custom_call" | custom-call | tf_op jit(solution)/shard_map/triple_product/pallas_call | solution.py:253
  63.9 1.8 %copy.8 = f32[64,1536]{1,0:T(8,128)} copy(f32[64,1536]{1,0:T(8,128)} %triple_product.1) | data formatting | bytes 786432

commit v3 on v2

--- a/solution.py
+++ b/solution.py
@@ -23,8 +23,8 @@
 def kernel(
     row_count, col_count, a_hbm, p_ref, ac_ref, pc_ref, sl_ref, out_ref,
     a_vm, send, send_cols, recv, recv_cols, dense, rt, prod,
-    pair_send, pair_recv, kept, line_send, line_recv,
-    a_sem, tile_ss, tile_rs, cols_ss, cols_rs, pair_ss, pair_rs, line_ss, line_rs,
+    pair_send, pair_recv, kept, line_send, combo, line_recv,
+    a_sem, tile_ss, tile_rs, cols_ss, cols_rs, pair_ss, pair_rs, line_ss, combo_rs, line_rs,
 ):
     g, c = lax.axis_index("row"), lax.axis_index("col")
     chips = col_count // 2
@@ -36,6 +36,8 @@
     wide = CG * bs
     piece = wide // col_count
     half = wide // 2
+    couple = z // 2
+    buddy = z + 1 - 2 * (z % 2)
     f32, bf16 = jnp.float32, jnp.bfloat16
 
     def group_ok(group):
@@ -62,7 +64,7 @@
 
     def pattern(r):
         lane = lax.broadcasted_iota(jnp.int32, (1, 2 * bs), 1)
-        return jnp.where(lane < bs, pc_ref[r, 0], pc_ref[r, 1])
+        return jnp.where(lane < bs, pc_ref[0, r], pc_ref[1, r])
 
     @pl.loop(0, col_count)
     def _(other):
@@ -98,11 +100,18 @@
             device_id=(g, 2 * z + 1 - k), device_id_type=MESH,
         )
 
-    def line_copy(w, source, target, other):
-        return pltpu.make_async_remote_copy(
-            src_ref=line_send.at[w, source], dst_ref=line_recv.at[w, target],
-            send_sem=line_ss.at[w, source], recv_sem=line_rs.at[w, target],
+    def line_copy(w, block, target, other):
+        return pltpu.make_async_remote_copy(
+            src_ref=line_send.at[w, block], dst_ref=line_recv.at[w, target],
+            send_sem=line_ss.at[w, block], recv_sem=line_rs.at[w, target],
             device_id=(g, 2 * other + k), device_id_type=MESH,
+        )
+
+    def combo_copy(w, block):
+        return pltpu.make_async_remote_copy(
+            src_ref=line_send.at[w, block], dst_ref=combo.at[w, block],
+            send_sem=line_ss.at[w, block], recv_sem=combo_rs.at[w, block],
+            device_id=(g, 2 * buddy + k), device_id_type=MESH,
         )
 
     for t in ORDER:
@@ -135,8 +144,8 @@
         first = p_ref[r, 0].astype(f32).T
         second = p_ref[r, 1].astype(f32).T
         for m in range(CG):
-            in_first = jnp.where(pc_ref[r, 0] == m, 1.0, 0.0)
-            in_second = jnp.where(pc_ref[r, 1] == m, 1.0, 0.0)
+            in_first = jnp.where(pc_ref[0, r] == m, 1.0, 0.0)
+            in_second = jnp.where(pc_ref[1, r] == m, 1.0, 0.0)
             block = (first * in_first + second * in_second).astype(bf16)
             for u in range(owners):
                 start = (u % 2) * half + (m * (owners // 2) + u // 2) * piece
@@ -161,8 +170,8 @@
                 def _():
                     spread(own + slot, send.at[slot], send_cols[slot])
 
-    def products(w):
-        @pl.loop(0, own)
+    def products(w, low, high):
+        @pl.loop(low, high)
         def _(i):
             index = []
             for s in range(slots):
@@ -185,46 +194,75 @@
         rows = rt[pl.ds(pl.multiple_of(core * half, half), half), :]
         return jnp.dot(rows, prod[...], preferred_element_type=f32)
 
-    def line_stage(w):
+    def block_rows(other):
+        return pl.ds(pl.multiple_of(other * piece, piece), piece)
+
+    def beyond_buddy(other):
+        return jnp.where(z % 2 == 0, other > z + 1, other < z - 1)
+
+    def beyond_self(other):
+        return jnp.where(z % 2 == 0, other < z, other > z)
+
+    def give(w):
         pair_copy(w).wait_recv()
-        columns = slice(w * wide, (w + 1) * wide)
+        kept[w] = kept[w] + pair_recv[w]
+        out_ref[:, w * wide : (w + 1) * wide] = kept[w, block_rows(z)]
 
         @pl.loop(0, chips)
         def _(step):
             other = far_first(z, chips, step)
-            rows = pl.ds(pl.multiple_of(other * piece, piece), piece)
-
-            @pl.when(other != z)
-            def _():
-                line_send[w, other] = (kept[w, rows] + pair_recv[w, rows]).astype(bf16)
-                line_copy(w, other, z, other).start()
-
-            @pl.when(other == z)
-            def _():
-                out_ref[:, columns] = kept[w, rows] + pair_recv[w, rows]
+
+            @pl.when(beyond_buddy(other))
+            def _():
+                line_send[w, other] = kept[w, block_rows(other)].astype(bf16)
+                combo_copy(w, other).start()
+
+        line_send[w, buddy] = kept[w, block_rows(buddy)].astype(bf16)
+        line_copy(w, buddy, couple, buddy).start()
+
+    def pass_on(w):
+        @pl.loop(0, chips)
+        def _(step):
+            other = far_first(z, chips, step)
+
+            @pl.when(beyond_self(other))
+            def _():
+                combo_copy(w, other).wait_recv()
+                total = kept[w, block_rows(other)] + combo[w, other].astype(f32)
+                line_send[w, other] = total.astype(bf16)
+                line_copy(w, other, couple, other).start()
 
     for s in range(slots):
         a_copy(s).wait()
     for n, w in enumerate(ORDER):
         take_stream(w)
-        if n == 2:
-            line_stage(ORDER[0])
-            line_stage(ORDER[1])
-        products(w)
+        if n < 2:
+            products(w, 0, own)
+        else:
+            pass_on(ORDER[0])
+            give(ORDER[1])
+            products(w, 0, own // 2)
+            pass_on(ORDER[1])
+            products(w, own // 2, own)
         pair_send[w] = restrict(1 - k)
         pair_copy(w).start()
         kept[w] = restrict(k)
-    line_stage(ORDER[2])
+        if n == 1:
+            give(ORDER[0])
+    give(ORDER[2])
+    pass_on(ORDER[2])
 
     for w in ORDER:
         columns = slice(w * wide, (w + 1) * wide)
 
+        @pl.loop(0, chips // 2)
+        def _(source):
+            line_copy(w, buddy, source, buddy).wait_recv()
+            out_ref[:, columns] += line_recv[w, source].astype(f32)
+
         @pl.loop(1, chips)
         def _(step):
-            other = (z + step) % chips
-            line_copy(w, other, other, other).wait_recv()
-            out_ref[:, columns] += line_recv[w, other].astype(f32)
-            line_copy(w, other, other, other).wait_send()
+            line_copy(w, (z + step) % chips, couple, buddy).wait_send()
 
         pair_copy(w).wait_send()
 
@@ -269,15 +307,16 @@
             pltpu.VMEM((3, wide // 2, wide), f32),
             pltpu.VMEM((3, chips, piece, wide), bf16),
             pltpu.VMEM((3, chips, piece, wide), bf16),
+            pltpu.VMEM((3, chips // 2, piece, wide), bf16),
             dma((slots,)),
             dma((ghosts,)), dma((ghosts,)), dma((ghosts,)), dma((ghosts,)),
-            dma((3,)), dma((3,)), dma((3, chips)), dma((3, chips)),
+            dma((3,)), dma((3,)), dma((3, chips)), dma((3, chips)), dma((3, chips // 2)),
         ],
         compiler_params=pltpu.CompilerParams(
             collective_id=0, has_side_effects=True, vmem_limit_bytes=VMEM_LIMIT
         ),
         name="triple_product",
-    )(a_tiles, p_tiles, a_cols, p_cols, send_list)
+    )(a_tiles, p_tiles, a_cols, p_cols.T, send_list)
 
 
 def solution(mesh):

time: 65.9 us -> 63 us (0.956)
  the two profiles are of different devices: /device:TPU:0 before, /device:TPU:5 now
where the time goes in v3:
time: 63 us; the launch traced here: 62.8 us
  Pallas kernels  61.1 us (97%)
  local copies, waits for them, and re-layouts  1.77 us (3%)
    pallas_call x1, Pallas kernels, body(): pl.pallas_call(functools.partial(kernel, row_count, col_count), out_shape...  61.1 us
    unnamed x1, local copies, waits for them, and re-layouts  1.77 us

profile of v3, /device:TPU:5, one launch (start us, length us, event | category | flops | bytes accessed | tf_op | source)
XLA Modules:
  0.0 62.8 jit_solution(17515520299574613334)
XLA Ops:
  0.0 61.1 %triple_product.1 = f32[64,1536]{1,0:T(8,128)} custom-call(bf16[8,16,128,128]{3,2,1,0:T(8,128)(2,1)} %a_hbm.1, bf16[8,2,128,128]{3,2,1,0:T(8,128)(2,1)} %p_ref.1, s32[8,16]{1,0:T(8,128)} %ac_ref.1, s32[2,8]{1,0:T(2,128)} %bitcast.1, s32[1,24]{1,0:T(1,128)} %sl_ref.1), custom_call_target="tpu_custom_call" | custom-call | tf_op jit(solution)/shard_map/triple_product/pallas_call | solution.py:291
  61.1 1.8 %copy.7 = f32[64,1536]{1,0:T(8,128)} copy(f32[64,1536]{1,0:T(8,128)} %triple_product.1) | data formatting | bytes 786432

commit v4 on v3

--- a/solution.py
+++ b/solution.py
@@ -114,7 +114,7 @@
             device_id=(g, 2 * buddy + k), device_id_type=MESH,
         )
 
-    for t in ORDER:
+    def start_stream(t):
         group = g + 1 - t
 
         @pl.loop(0, col_count)
@@ -125,6 +125,21 @@
             def _():
                 cols_copy(other * 3 + t, c * 3 + t, group, other).start()
                 tiles_copy(other * 3 + t, c * 3 + t, group, other).start()
+
+    def finish_stream(t):
+        group = g + 1 - t
+
+        @pl.loop(0, col_count)
+        def _(other):
+            slot = other * 3 + t
+
+            @pl.when(group_ok(group) & ((other != c) | (t != 1)))
+            def _():
+                cols_copy(slot, slot, group, other).wait_send()
+                tiles_copy(slot, slot, group, other).wait_send()
+
+    start_stream(ORDER[0])
+    start_stream(ORDER[1])
 
     def spread(target, tiles, cols):
         first, second = tiles[0].astype(f32), tiles[1].astype(f32)
@@ -236,6 +251,9 @@
         a_copy(s).wait()
     for n, w in enumerate(ORDER):
         take_stream(w)
+        finish_stream(w)
+        if n == 0:
+            start_stream(ORDER[2])
         if n < 2:
             products(w, 0, own)
         else:
@@ -265,15 +283,6 @@
             line_copy(w, (z + step) % chips, couple, buddy).wait_send()
 
         pair_copy(w).wait_send()
-
-        @pl.loop(0, col_count)
-        def _(other):
-            slot = other * 3 + w
-
-            @pl.when(group_ok(g + 1 - w) & ((other != c) | (w != 1)))
-            def _():
-                cols_copy(slot, slot, g + 1 - w, other).wait_send()
-                tiles_copy(slot, slot, g + 1 - w, other).wait_send()
 
 
 def body(row_count, col_count, a_tiles, a_cols, p_tiles, p_cols, send_list):

time: 63 us -> 63 us (level)
  no operation moved by 1% of the time
where the time goes in v4:
time: 63 us; the launch traced here: 62.3 us
  Pallas kernels  60.5 us (96%)
  local copies, waits for them, and re-layouts  1.77 us (3%)
    pallas_call x1, Pallas kernels, body(): pl.pallas_call(functools.partial(kernel, row_count, col_count), out_shape...  60.5 us
    unnamed x1, local copies, waits for them, and re-layouts  1.77 us

profile of v4, /device:TPU:5, one launch (start us, length us, event | category | flops | bytes accessed | tf_op | source)
XLA Modules:
  0.0 62.3 jit_solution(16848761094215744959)
XLA Ops:
  0.0 60.5 %triple_product.1 = f32[64,1536]{1,0:T(8,128)} custom-call(bf16[8,16,128,128]{3,2,1,0:T(8,128)(2,1)} %a_hbm.1, bf16[8,2,128,128]{3,2,1,0:T(8,128)(2,1)} %p_ref.1, s32[8,16]{1,0:T(8,128)} %ac_ref.1, s32[2,8]{1,0:T(2,128)} %bitcast.1, s32[1,24]{1,0:T(1,128)} %sl_ref.1), custom_call_target="tpu_custom_call" | custom-call | tf_op jit(solution)/shard_map/triple_product/pallas_call | solution.py:300
  60.5 1.8 %copy.7 = f32[64,1536]{1,0:T(8,128)} copy(f32[64,1536]{1,0:T(8,128)} %triple_product.1) | data formatting | bytes 786432

commit v5 on v4

--- a/solution.py
+++ b/solution.py
@@ -22,7 +22,7 @@
 
 def kernel(
     row_count, col_count, a_hbm, p_ref, ac_ref, pc_ref, sl_ref, out_ref,
-    a_vm, send, send_cols, recv, recv_cols, dense, rt, prod,
+    a_vm, chain, a_first, a_other, following, send, send_cols, recv, recv_cols, dense, rt, prod,
     pair_send, pair_recv, kept, line_send, combo, line_recv,
     a_sem, tile_ss, tile_rs, cols_ss, cols_rs, pair_ss, pair_rs, line_ss, combo_rs, line_rs,
 ):
@@ -32,7 +32,6 @@
     own, slots = ac_ref.shape
     bs = p_ref.shape[-1]
     ghosts = 3 * col_count
-    zero_row = own + ghosts
     wide = CG * bs
     piece = wide // col_count
     half = wide // 2
@@ -43,11 +42,7 @@
     def group_ok(group):
         return (group >= 0) & (group < row_count)
 
-    def a_copy(s):
-        return pltpu.make_async_copy(
-            a_hbm.at[:, s], a_vm.at[:, :, pl.ds(s * bs, bs)], a_sem.at[s]
-        )
-
+    a_copy = pltpu.make_async_copy(a_hbm, a_vm, a_sem)
     barrier = pltpu.get_barrier_semaphore()
 
     @pl.loop(0, col_count)
@@ -59,8 +54,7 @@
             def _():
                 pl.semaphore_signal(barrier, inc=1, device_id=(group, other), device_id_type=MESH)
 
-    for s in range(slots):
-        a_copy(s).start()
+    a_copy.start()
 
     def pattern(r):
         lane = lax.broadcasted_iota(jnp.int32, (1, 2 * bs), 1)
@@ -138,24 +132,23 @@
                 cols_copy(slot, slot, group, other).wait_send()
                 tiles_copy(slot, slot, group, other).wait_send()
 
-    start_stream(ORDER[0])
-    start_stream(ORDER[1])
+    for t in ORDER:
+        start_stream(t)
 
     def spread(target, tiles, cols):
         first, second = tiles[0].astype(f32), tiles[1].astype(f32)
         for m in range(CG):
             in_first = jnp.where(cols[:, :bs] == m, 1.0, 0.0)
             in_second = jnp.where(cols[:, bs:] == m, 1.0, 0.0)
-            dense[target, :, m * bs : (m + 1) * bs] = (
+            dense[pl.ds(pl.multiple_of(target * bs, bs), bs), m * bs : (m + 1) * bs] = (
                 first * in_first + second * in_second
             ).astype(bf16)
 
-    dense[zero_row] = jnp.zeros((bs, wide), bf16)
     owners = col_count // CG
 
     @pl.loop(0, own)
     def _(r):
-        spread(r, p_ref.at[r], pattern(r))
+        spread(col_count + r, p_ref.at[r], pattern(r))
         first = p_ref[r, 0].astype(f32).T
         second = p_ref[r, 1].astype(f32).T
         for m in range(CG):
@@ -177,33 +170,59 @@
             def _():
                 cols_copy(slot, slot, g + t - 1, other).wait_recv()
                 tiles_copy(slot, slot, g + t - 1, other).wait_recv()
-                spread(own + slot, recv.at[slot], recv_cols[slot])
+                spread(other, recv.at[slot], recv_cols[slot])
 
             if t == 1:
 
                 @pl.when(other == c)
                 def _():
-                    spread(own + slot, send.at[slot], send_cols[slot])
-
-    def products(w, low, high):
+                    spread(other, send.at[slot], send_cols[slot])
+
+    @pl.loop(0, own)
+    def _(i):
+        for s in range(slots):
+            after = jnp.int32(slots)
+            for later in range(slots - 1, s, -1):
+                after = jnp.where(ac_ref[i, later] == ac_ref[i, s], later, after)
+            following[i, s] = after
+
+    chain[slots] = jnp.zeros((bs, bs), f32)
+
+    def lay_out(parts):
+        @pl.loop(0, own)
+        def _(i):
+            for s in range(slots - 1, -1, -1):
+                chain[s] = a_vm[i, s].astype(f32) + chain[following[i, s]]
+            rows = pl.ds(pl.multiple_of(i * bs, bs), bs)
+
+            def place(target, position, b):
+                first = jnp.int32(slots)
+                for s in range(slots - 1, -1, -1):
+                    first = jnp.where(ac_ref[i, s] == b, s, first)
+                columns = pl.ds(pl.multiple_of(position * bs, bs), bs)
+                target[rows, columns] = chain[first].astype(bf16)
+
+            for t, target in parts:
+
+                @pl.loop(0, col_count)
+                def _(q):
+                    place(target, q, own + 3 * q + t)
+
+                if t == 1:
+
+                    @pl.loop(0, own)
+                    def _(r):
+                        place(target, col_count + r, r)
+
+    def products(a_part, depth, low, high):
+        step_rows = 2 * bs
+
         @pl.loop(low, high)
-        def _(i):
-            index = []
-            for s in range(slots):
-                b = ac_ref[i, s]
-                ghost = jnp.maximum(b - own, 0)
-                stream = jnp.where(b < own, 1, ghost % 3)
-                index.append(jnp.where((b >= 0) & (stream == w), b, zero_row))
-            for n in range(0, wide, 2 * bs):
-                total = jnp.zeros((bs, 2 * bs), f32)
-                for s in range(0, slots, 2):
-                    right = jnp.concatenate(
-                        [dense[index[s], :, n : n + 2 * bs], dense[index[s + 1], :, n : n + 2 * bs]],
-                        axis=0,
-                    )
-                    left = a_vm[i, :, s * bs : (s + 2) * bs]
-                    total = total + jnp.dot(left, right, preferred_element_type=f32)
-                prod[pl.ds(pl.multiple_of(i * bs, bs), bs), n : n + 2 * bs] = total.astype(bf16)
+        def _(step):
+            rows = pl.ds(pl.multiple_of(step * step_rows, step_rows), step_rows)
+            prod[rows, :] = jnp.dot(
+                a_part[rows, :depth], dense[:depth, :], preferred_element_type=f32
+            ).astype(bf16)
 
     def restrict(core):
         rows = rt[pl.ds(pl.multiple_of(core * half, half), half), :]
@@ -247,24 +266,27 @@
                 line_send[w, other] = total.astype(bf16)
                 line_copy(w, other, couple, other).start()
 
-    for s in range(slots):
-        a_copy(s).wait()
+    a_copy.wait()
+    lay_out(((1, a_first), (0, a_other)))
+    steps = own // 2
+    ghost_depth = col_count * bs
     for n, w in enumerate(ORDER):
         take_stream(w)
-        finish_stream(w)
         if n == 0:
-            start_stream(ORDER[2])
-        if n < 2:
-            products(w, 0, own)
+            products(a_first, ghost_depth + own * bs, 0, steps)
+        elif n == 1:
+            products(a_other, ghost_depth, 0, steps)
         else:
             pass_on(ORDER[0])
             give(ORDER[1])
-            products(w, 0, own // 2)
+            products(a_first, ghost_depth, 0, steps // 2)
             pass_on(ORDER[1])
-            products(w, own // 2, own)
+            products(a_first, ghost_depth, steps // 2, steps)
         pair_send[w] = restrict(1 - k)
         pair_copy(w).start()
         kept[w] = restrict(k)
+        if n == 0:
+            lay_out(((2, a_first),))
         if n == 1:
             give(ORDER[0])
     give(ORDER[2])
@@ -283,6 +305,7 @@
             line_copy(w, (z + step) % chips, couple, buddy).wait_send()
 
         pair_copy(w).wait_send()
+        finish_stream(w)
 
 
 def body(row_count, col_count, a_tiles, a_cols, p_tiles, p_cols, send_list):
@@ -303,12 +326,16 @@
         in_specs=[pl.BlockSpec(memory_space=pl.ANY), vmem, smem, smem, smem],
         out_specs=vmem,
         scratch_shapes=[
-            pltpu.VMEM((own, bs, slots * bs), bf16),
+            pltpu.VMEM((own, slots, bs, bs), bf16),
+            pltpu.VMEM((slots + 1, bs, bs), f32),
+            pltpu.VMEM((own * bs, (col_count + own) * bs), bf16),
+            pltpu.VMEM((own * bs, col_count * bs), bf16),
+            pltpu.SMEM((own, slots), jnp.int32),
             pltpu.VMEM((ghosts, tiles, bs, bs), bf16),
             pltpu.VMEM((ghosts, 1, tiles * bs), jnp.int32),
             pltpu.VMEM((ghosts, tiles, bs, bs), bf16),
             pltpu.VMEM((ghosts, 1, tiles * bs), jnp.int32),
-            pltpu.VMEM((own + ghosts + 1, bs, wide), bf16),
+            pltpu.VMEM(((col_count + own) * bs, wide), bf16),
             pltpu.VMEM((wide, own * bs), bf16),
             pltpu.VMEM((own * bs, wide), bf16),
             pltpu.VMEM((3, wide // 2, wide), f32),
@@ -317,7 +344,7 @@
             pltpu.VMEM((3, chips, piece, wide), bf16),
             pltpu.VMEM((3, chips, piece, wide), bf16),
             pltpu.VMEM((3, chips // 2, piece, wide), bf16),
-            dma((slots,)),
+            dma,
             dma((ghosts,)), dma((ghosts,)), dma((ghosts,)), dma((ghosts,)),
             dma((3,)), dma((3,)), dma((3, chips)), dma((3, chips)), dma((3, chips // 2)),
         ],

time: 63 us -> 60.6 us (0.962)
  Pallas kernels: 60.5 us -> 58.4 us
    pallas_call x1, Pallas kernels: 60.5 us -> 58.4 us  [body(): pl.pallas_call(functools.partial(kernel, row_count, col_count), out_shape...]
where the time goes in v5:
time: 60.6 us; the launch traced here: 60.2 us
  Pallas kernels  58.4 us (96%)
  local copies, waits for them, and re-layouts  1.77 us (3%)
    pallas_call x1, Pallas kernels, body(): pl.pallas_call(functools.partial(kernel, row_count, col_count), out_shape...  58.4 us
    unnamed x1, local copies, waits for them, and re-layouts  1.77 us

profile of v5, /device:TPU:5, one launch (start us, length us, event | category | flops | bytes accessed | tf_op | source)
XLA Modules:
  0.0 60.2 jit_solution(1604904844301330786)
XLA Ops:
  0.0 58.4 %triple_product.1 = f32[64,1536]{1,0:T(8,128)} custom-call(bf16[8,16,128,128]{3,2,1,0:T(8,128)(2,1)} %a_hbm.1, bf16[8,2,128,128]{3,2,1,0:T(8,128)(2,1)} %p_ref.1, s32[8,16]{1,0:T(8,128)} %ac_ref.1, s32[2,8]{1,0:T(2,128)} %bitcast.1, s32[1,24]{1,0:T(1,128)} %sl_ref.1), custom_call_target="tpu_custom_call" | custom-call | tf_op jit(solution)/shard_map/triple_product/pallas_call | solution.py:323
  58.5 1.8 %copy.7 = f32[64,1536]{1,0:T(8,128)} copy(f32[64,1536]{1,0:T(8,128)} %triple_product.1) | data formatting | bytes 786432

commit v6 on v5

--- a/solution.py
+++ b/solution.py
@@ -22,7 +22,7 @@
 
 def kernel(
     row_count, col_count, a_hbm, p_ref, ac_ref, pc_ref, sl_ref, out_ref,
-    a_vm, chain, a_first, a_other, following, send, send_cols, recv, recv_cols, dense, rt, prod,
+    a_vm, chain, a_high, a_low, following, send, send_cols, recv, recv_cols, dense, rt, prod,
     pair_send, pair_recv, kept, line_send, combo, line_recv,
     a_sem, tile_ss, tile_rs, cols_ss, cols_rs, pair_ss, pair_rs, line_ss, combo_rs, line_rs,
 ):
@@ -132,8 +132,8 @@
                 cols_copy(slot, slot, group, other).wait_send()
                 tiles_copy(slot, slot, group, other).wait_send()
 
-    for t in ORDER:
-        start_stream(t)
+    start_stream(ORDER[0])
+    start_stream(ORDER[1])
 
     def spread(target, tiles, cols):
         first, second = tiles[0].astype(f32), tiles[1].astype(f32)
@@ -188,41 +188,44 @@
 
     chain[slots] = jnp.zeros((bs, bs), f32)
 
-    def lay_out(parts):
+    def lay_out(t):
         @pl.loop(0, own)
         def _(i):
             for s in range(slots - 1, -1, -1):
                 chain[s] = a_vm[i, s].astype(f32) + chain[following[i, s]]
             rows = pl.ds(pl.multiple_of(i * bs, bs), bs)
 
-            def place(target, position, b):
+            def place(position, b):
                 first = jnp.int32(slots)
                 for s in range(slots - 1, -1, -1):
                     first = jnp.where(ac_ref[i, s] == b, s, first)
                 columns = pl.ds(pl.multiple_of(position * bs, bs), bs)
-                target[rows, columns] = chain[first].astype(bf16)
-
-            for t, target in parts:
-
-                @pl.loop(0, col_count)
-                def _(q):
-                    place(target, q, own + 3 * q + t)
-
-                if t == 1:
-
-                    @pl.loop(0, own)
-                    def _(r):
-                        place(target, col_count + r, r)
-
-    def products(a_part, depth, low, high):
+                total = chain[first]
+                high = total.astype(bf16)
+                a_high[rows, columns] = high
+                a_low[rows, columns] = (total - high.astype(f32)).astype(bf16)
+
+            @pl.loop(0, col_count)
+            def _(q):
+                place(q, own + 3 * q + t)
+
+            if t == 1:
+
+                @pl.loop(0, own)
+                def _(r):
+                    place(col_count + r, r)
+
+    def products(w):
         step_rows = 2 * bs
-
-        @pl.loop(low, high)
+        depth = (col_count + (own if w == 1 else 0)) * bs
+
+        @pl.loop(0, own // 2)
         def _(step):
             rows = pl.ds(pl.multiple_of(step * step_rows, step_rows), step_rows)
-            prod[rows, :] = jnp.dot(
-                a_part[rows, :depth], dense[:depth, :], preferred_element_type=f32
-            ).astype(bf16)
+            right = dense[:depth, :]
+            total = jnp.dot(a_high[rows, :depth], right, preferred_element_type=f32)
+            total = total + jnp.dot(a_low[rows, :depth], right, preferred_element_type=f32)
+            prod[rows, :] = total.astype(bf16)
 
     def restrict(core):
         rows = rt[pl.ds(pl.multiple_of(core * half, half), half), :]
@@ -254,6 +257,23 @@
         line_send[w, buddy] = kept[w, block_rows(buddy)].astype(bf16)
         line_copy(w, buddy, couple, buddy).start()
 
+    def give_straight(w):
+        pair_copy(w).wait_recv()
+
+        @pl.loop(0, chips)
+        def _(step):
+            other = far_first(z, chips, step)
+
+            @pl.when(other != z)
+            def _():
+                total = kept[w, block_rows(other)] + pair_recv[w, block_rows(other)]
+                line_send[w, other] = total.astype(bf16)
+                line_copy(w, other, z, other).start()
+
+        out_ref[:, w * wide : (w + 1) * wide] = (
+            kept[w, block_rows(z)] + pair_recv[w, block_rows(z)]
+        )
+
     def pass_on(w):
         @pl.loop(0, chips)
         def _(step):
@@ -267,36 +287,31 @@
                 line_copy(w, other, couple, other).start()
 
     a_copy.wait()
-    lay_out(((1, a_first), (0, a_other)))
-    steps = own // 2
-    ghost_depth = col_count * bs
+    lay_out(ORDER[0])
     for n, w in enumerate(ORDER):
         take_stream(w)
         if n == 0:
-            products(a_first, ghost_depth + own * bs, 0, steps)
-        elif n == 1:
-            products(a_other, ghost_depth, 0, steps)
-        else:
-            pass_on(ORDER[0])
-            give(ORDER[1])
-            products(a_first, ghost_depth, 0, steps // 2)
-            pass_on(ORDER[1])
-            products(a_first, ghost_depth, steps // 2, steps)
+            finish_stream(w)
+            start_stream(ORDER[2])
+        products(w)
         pair_send[w] = restrict(1 - k)
         pair_copy(w).start()
         kept[w] = restrict(k)
-        if n == 0:
-            lay_out(((2, a_first),))
+        if n < 2:
+            lay_out(ORDER[n + 1])
         if n == 1:
             give(ORDER[0])
-    give(ORDER[2])
-    pass_on(ORDER[2])
-
-    for w in ORDER:
+            pass_on(ORDER[0])
+            give(ORDER[1])
+            pass_on(ORDER[1])
+    give_straight(ORDER[2])
+
+    for n, w in enumerate(ORDER):
         columns = slice(w * wide, (w + 1) * wide)
 
-        @pl.loop(0, chips // 2)
-        def _(source):
+        @pl.loop(0, chips // 2 if n < 2 else chips - 1)
+        def _(step):
+            source = step if n < 2 else (z + 1 + step) % chips
             line_copy(w, buddy, source, buddy).wait_recv()
             out_ref[:, columns] += line_recv[w, source].astype(f32)
 
@@ -304,8 +319,9 @@
         def _(step):
             line_copy(w, (z + step) % chips, couple, buddy).wait_send()
 
+        if n > 0:
+            finish_stream(w)
         pair_copy(w).wait_send()
-        finish_stream(w)
 
 
 def body(row_count, col_count, a_tiles, a_cols, p_tiles, p_cols, send_list):
@@ -329,7 +345,7 @@
             pltpu.VMEM((own, slots, bs, bs), bf16),
             pltpu.VMEM((slots + 1, bs, bs), f32),
             pltpu.VMEM((own * bs, (col_count + own) * bs), bf16),
-            pltpu.VMEM((own * bs, col_count * bs), bf16),
+            pltpu.VMEM((own * bs, (col_count + own) * bs), bf16),
             pltpu.SMEM((own, slots), jnp.int32),
             pltpu.VMEM((ghosts, tiles, bs, bs), bf16),
             pltpu.VMEM((ghosts, 1, tiles * bs), jnp.int32),
@@ -343,10 +359,10 @@
             pltpu.VMEM((3, wide // 2, wide), f32),
             pltpu.VMEM((3, chips, piece, wide), bf16),
             pltpu.VMEM((3, chips, piece, wide), bf16),
-            pltpu.VMEM((3, chips // 2, piece, wide), bf16),
+            pltpu.VMEM((3, chips, piece, wide), bf16),
             dma,
             dma((ghosts,)), dma((ghosts,)), dma((ghosts,)), dma((ghosts,)),
-            dma((3,)), dma((3,)), dma((3, chips)), dma((3, chips)), dma((3, chips // 2)),
+            dma((3,)), dma((3,)), dma((3, chips)), dma((3, chips)), dma((3, chips)),
         ],
         compiler_params=pltpu.CompilerParams(
             collective_id=0, has_side_effects=True, vmem_limit_bytes=VMEM_LIMIT

time: 60.6 us -> 65.3 us (1.078)
  Pallas kernels: 58.4 us -> 63.4 us
    pallas_call x1, Pallas kernels: 58.4 us -> 63.4 us  [body(): pl.pallas_call(functools.partial(kernel, row_count, col_count), out_shape...]
where the time goes in v6:
time: 65.3 us; the launch traced here: 65.1 us
  Pallas kernels  63.4 us (97%)
  local copies, waits for them, and re-layouts  1.77 us (3%)
    pallas_call x1, Pallas kernels, body(): pl.pallas_call(functools.partial(kernel, row_count, col_count), out_shape...  63.4 us
    unnamed x1, local copies, waits for them, and re-layouts  1.77 us

profile of v6, /device:TPU:5, one launch (start us, length us, event | category | flops | bytes accessed | tf_op | source)
XLA Modules:
  0.0 65.1 jit_solution(6687120211113291151)
XLA Ops:
  0.0 63.4 %triple_product.1 = f32[64,1536]{1,0:T(8,128)} custom-call(bf16[8,16,128,128]{3,2,1,0:T(8,128)(2,1)} %a_hbm.1, bf16[8,2,128,128]{3,2,1,0:T(8,128)(2,1)} %p_ref.1, s32[8,16]{1,0:T(8,128)} %ac_ref.1, s32[2,8]{1,0:T(2,128)} %bitcast.1, s32[1,24]{1,0:T(1,128)} %sl_ref.1), custom_call_target="tpu_custom_call" | custom-call | tf_op jit(solution)/shard_map/triple_product/pallas_call | solution.py:339
  63.4 1.8 %copy.7 = f32[64,1536]{1,0:T(8,128)} copy(f32[64,1536]{1,0:T(8,128)} %triple_product.1) | data formatting | bytes 786432

commit v7 on v6

--- a/solution.py
+++ b/solution.py
@@ -132,8 +132,8 @@
                 cols_copy(slot, slot, group, other).wait_send()
                 tiles_copy(slot, slot, group, other).wait_send()
 
-    start_stream(ORDER[0])
-    start_stream(ORDER[1])
+    for t in ORDER:
+        start_stream(t)
 
     def spread(target, tiles, cols):
         first, second = tiles[0].astype(f32), tiles[1].astype(f32)
@@ -202,8 +202,8 @@
                 columns = pl.ds(pl.multiple_of(position * bs, bs), bs)
                 total = chain[first]
                 high = total.astype(bf16)
-                a_high[rows, columns] = high
-                a_low[rows, columns] = (total - high.astype(f32)).astype(bf16)
+                a_high[t % a_high.shape[0], rows, columns] = high
+                a_low[t % a_low.shape[0], rows, columns] = (total - high.astype(f32)).astype(bf16)
 
             @pl.loop(0, col_count)
             def _(q):
@@ -215,16 +215,16 @@
                 def _(r):
                     place(col_count + r, r)
 
-    def products(w):
+    def products(w, low, high):
         step_rows = 2 * bs
         depth = (col_count + (own if w == 1 else 0)) * bs
 
-        @pl.loop(0, own // 2)
+        @pl.loop(low, high)
         def _(step):
             rows = pl.ds(pl.multiple_of(step * step_rows, step_rows), step_rows)
             right = dense[:depth, :]
-            total = jnp.dot(a_high[rows, :depth], right, preferred_element_type=f32)
-            total = total + jnp.dot(a_low[rows, :depth], right, preferred_element_type=f32)
+            total = jnp.dot(a_high[w % a_high.shape[0], rows, :depth], right, preferred_element_type=f32)
+            total = total + jnp.dot(a_low[w % a_low.shape[0], rows, :depth], right, preferred_element_type=f32)
             prod[rows, :] = total.astype(bf16)
 
     def restrict(core):
@@ -287,23 +287,27 @@
                 line_copy(w, other, couple, other).start()
 
     a_copy.wait()
-    lay_out(ORDER[0])
+    roomy = a_high.shape[0] == 3
+    for w in ORDER if roomy else ORDER[:1]:
+        lay_out(w)
+    steps = own // 2
     for n, w in enumerate(ORDER):
         take_stream(w)
-        if n == 0:
-            finish_stream(w)
-            start_stream(ORDER[2])
-        products(w)
+        if n < 2:
+            products(w, 0, steps)
+        else:
+            pass_on(ORDER[0])
+            give(ORDER[1])
+            products(w, 0, steps // 2)
+            pass_on(ORDER[1])
+            products(w, steps // 2, steps)
         pair_send[w] = restrict(1 - k)
         pair_copy(w).start()
         kept[w] = restrict(k)
-        if n < 2:
+        if n < 2 and not roomy:
             lay_out(ORDER[n + 1])
         if n == 1:
             give(ORDER[0])
-            pass_on(ORDER[0])
-            give(ORDER[1])
-            pass_on(ORDER[1])
     give_straight(ORDER[2])
 
     for n, w in enumerate(ORDER):
@@ -319,8 +323,7 @@
         def _(step):
             line_copy(w, (z + step) % chips, couple, buddy).wait_send()
 
-        if n > 0:
-            finish_stream(w)
+        finish_stream(w)
         pair_copy(w).wait_send()
 
 
@@ -332,6 +335,7 @@
     chips = col_count // 2
     wide = CG * bs
     piece = wide // col_count
+    layouts = 3 if col_count <= own else 1
     vmem = pl.BlockSpec(memory_space=pltpu.VMEM)
     smem = pl.BlockSpec(memory_space=pltpu.SMEM)
     dma = pltpu.SemaphoreType.DMA
@@ -344,8 +348,8 @@
         scratch_shapes=[
             pltpu.VMEM((own, slots, bs, bs), bf16),
             pltpu.VMEM((slots + 1, bs, bs), f32),
-            pltpu.VMEM((own * bs, (col_count + own) * bs), bf16),
-            pltpu.VMEM((own * bs, (col_count + own) * bs), bf16),
+            pltpu.VMEM((layouts, own * bs, (col_count + own) * bs), bf16),
+            pltpu.VMEM((layouts, own * bs, (col_count + own) * bs), bf16),
             pltpu.SMEM((own, slots), jnp.int32),
             pltpu.VMEM((ghosts, tiles, bs, bs), bf16),
             pltpu.VMEM((ghosts, 1, tiles * bs), jnp.int32),

time: 65.3 us -> 61.8 us (0.946)
  Pallas kernels: 63.4 us -> 59.8 us
    pallas_call x1, Pallas kernels: 63.4 us -> 59.8 us  [body(): pl.pallas_call(functools.partial(kernel, row_count, col_count), out_shape...]
where the time goes in v7:
time: 61.8 us; the launch traced here: 61.6 us
  Pallas kernels  59.8 us (97%)
  local copies, waits for them, and re-layouts  1.77 us (3%)
    pallas_call x1, Pallas kernels, body(): pl.pallas_call(functools.partial(kernel, row_count, col_count), out_shape...  59.8 us
    unnamed x1, local copies, waits for them, and re-layouts  1.77 us

profile of v7, /device:TPU:5, one launch (start us, length us, event | category | flops | bytes accessed | tf_op | source)
XLA Modules:
  0.0 61.6 jit_solution(2712207196498054740)
XLA Ops:
  0.0 59.8 %triple_product.1 = f32[64,1536]{1,0:T(8,128)} custom-call(bf16[8,16,128,128]{3,2,1,0:T(8,128)(2,1)} %a_hbm.1, bf16[8,2,128,128]{3,2,1,0:T(8,128)(2,1)} %p_ref.1, s32[8,16]{1,0:T(8,128)} %ac_ref.1, s32[2,8]{1,0:T(2,128)} %bitcast.1, s32[1,24]{1,0:T(1,128)} %sl_ref.1), custom_call_target="tpu_custom_call" | custom-call | tf_op jit(solution)/shard_map/triple_product/pallas_call | solution.py:343
  59.8 1.8 %copy.7 = f32[64,1536]{1,0:T(8,128)} copy(f32[64,1536]{1,0:T(8,128)} %triple_product.1) | data formatting | bytes 786432

commit v8 on v7

--- a/solution.py
+++ b/solution.py
@@ -60,15 +60,16 @@
         lane = lax.broadcasted_iota(jnp.int32, (1, 2 * bs), 1)
         return jnp.where(lane < bs, pc_ref[0, r], pc_ref[1, r])
 
-    @pl.loop(0, col_count)
-    def _(other):
-        for t in range(3):
+    def gather(t):
+        @pl.loop(0, col_count)
+        def _(other):
             j = other * 3 + t
             r = sl_ref[0, j]
             send[j, 0] = p_ref[r, 0]
             send[j, 1] = p_ref[r, 1]
             send_cols[j] = pattern(r)
 
+    gather(ORDER[0])
     peers = col_count - 1
     peers = peers + jnp.where(g > 0, col_count, 0) + jnp.where(g < row_count - 1, col_count, 0)
     pl.semaphore_wait(barrier, peers)
@@ -132,7 +133,9 @@
                 cols_copy(slot, slot, group, other).wait_send()
                 tiles_copy(slot, slot, group, other).wait_send()
 
-    for t in ORDER:
+    for n, t in enumerate(ORDER):
+        if n > 0:
+            gather(t)
         start_stream(t)
 
     def spread(target, tiles, cols):
@@ -296,8 +299,6 @@
         if n < 2:
             products(w, 0, steps)
         else:
-            pass_on(ORDER[0])
-            give(ORDER[1])
             products(w, 0, steps // 2)
             pass_on(ORDER[1])
             products(w, steps // 2, steps)
@@ -308,6 +309,8 @@
             lay_out(ORDER[n + 1])
         if n == 1:
             give(ORDER[0])
+            give(ORDER[1])
+            pass_on(ORDER[0])
     give_straight(ORDER[2])
 
     for n, w in enumerate(ORDER):

time: 61.8 us -> 61.7 us (level)
  no operation moved by 1% of the time
where the time goes in v8:
time: 61.7 us; the launch traced here: 61.6 us
  Pallas kernels  59.8 us (97%)
  local copies, waits for them, and re-layouts  1.77 us (3%)
    pallas_call x1, Pallas kernels, body(): pl.pallas_call(functools.partial(kernel, row_count, col_count), out_shape...  59.8 us
    unnamed x1, local copies, waits for them, and re-layouts  1.77 us

profile of v8, /device:TPU:5, one launch (start us, length us, event | category | flops | bytes accessed | tf_op | source)
XLA Modules:
  0.0 61.6 jit_solution(16719923513548927202)
XLA Ops:
  0.0 59.8 %triple_product.1 = f32[64,1536]{1,0:T(8,128)} custom-call(bf16[8,16,128,128]{3,2,1,0:T(8,128)(2,1)} %a_hbm.1, bf16[8,2,128,128]{3,2,1,0:T(8,128)(2,1)} %p_ref.1, s32[8,16]{1,0:T(8,128)} %ac_ref.1, s32[2,8]{1,0:T(2,128)} %bitcast.1, s32[1,24]{1,0:T(1,128)} %sl_ref.1), custom_call_target="tpu_custom_call" | custom-call | tf_op jit(solution)/shard_map/triple_product/pallas_call | solution.py:346
  59.8 1.8 %copy.7 = f32[64,1536]{1,0:T(8,128)} copy(f32[64,1536]{1,0:T(8,128)} %triple_product.1) | data formatting | bytes 786432

commit v9 on v8

--- a/solution.py
+++ b/solution.py
@@ -22,7 +22,7 @@
 
 def kernel(
     row_count, col_count, a_hbm, p_ref, ac_ref, pc_ref, sl_ref, out_ref,
-    a_vm, chain, a_high, a_low, following, send, send_cols, recv, recv_cols, dense, rt, prod,
+    a_vm, chain, chain_high, chain_low, a_high, a_low, following, send, send_cols, recv, recv_cols, dense, rt, prod,
     pair_send, pair_recv, kept, line_send, combo, line_recv,
     a_sem, tile_ss, tile_rs, cols_ss, cols_rs, pair_ss, pair_rs, line_ss, combo_rs, line_rs,
 ):
@@ -191,32 +191,36 @@
 
     chain[slots] = jnp.zeros((bs, bs), f32)
 
-    def lay_out(t):
+    chain_high[slots] = jnp.zeros((bs, bs), bf16)
+    chain_low[slots] = jnp.zeros((bs, bs), bf16)
+
+    def lay_out(windows):
         @pl.loop(0, own)
         def _(i):
+            named = [ac_ref[i, s] for s in range(slots)]
             for s in range(slots - 1, -1, -1):
-                chain[s] = a_vm[i, s].astype(f32) + chain[following[i, s]]
+                total = a_vm[i, s].astype(f32) + chain[following[i, s]]
+                high = total.astype(bf16)
+                chain[s] = total
+                chain_high[s] = high
+                chain_low[s] = (total - high.astype(f32)).astype(bf16)
             rows = pl.ds(pl.multiple_of(i * bs, bs), bs)
 
-            def place(position, b):
+            def place(at, position, b):
                 first = jnp.int32(slots)
                 for s in range(slots - 1, -1, -1):
-                    first = jnp.where(ac_ref[i, s] == b, s, first)
-                columns = pl.ds(pl.multiple_of(position * bs, bs), bs)
-                total = chain[first]
-                high = total.astype(bf16)
-                a_high[t % a_high.shape[0], rows, columns] = high
-                a_low[t % a_low.shape[0], rows, columns] = (total - high.astype(f32)).astype(bf16)
-
-            @pl.loop(0, col_count)
-            def _(q):
-                place(q, own + 3 * q + t)
-
-            if t == 1:
-
-                @pl.loop(0, own)
-                def _(r):
-                    place(col_count + r, r)
+                    first = jnp.where(named[s] == b, s, first)
+                columns = slice(position * bs, (position + 1) * bs)
+                a_high[at, rows, columns] = chain_high[first]
+                a_low[at, rows, columns] = chain_low[first]
+
+            for t in windows:
+                at = t % a_high.shape[0]
+                for q in range(col_count):
+                    place(at, q, own + 3 * q + t)
+                if t == 1:
+                    for r in range(own):
+                        place(at, col_count + r, r)
 
     def products(w, low, high):
         step_rows = 2 * bs
@@ -291,8 +295,7 @@
 
     a_copy.wait()
     roomy = a_high.shape[0] == 3
-    for w in ORDER if roomy else ORDER[:1]:
-        lay_out(w)
+    lay_out(ORDER if roomy else ORDER[:1])
     steps = own // 2
     for n, w in enumerate(ORDER):
         take_stream(w)
@@ -306,7 +309,7 @@
         pair_copy(w).start()
         kept[w] = restrict(k)
         if n < 2 and not roomy:
-            lay_out(ORDER[n + 1])
+            lay_out(ORDER[n + 1 : n + 2])
         if n == 1:
             give(ORDER[0])
             give(ORDER[1])
@@ -351,6 +354,8 @@
         scratch_shapes=[
             pltpu.VMEM((own, slots, bs, bs), bf16),
             pltpu.VMEM((slots + 1, bs, bs), f32),
+            pltpu.VMEM((slots + 1, bs, bs), bf16),
+            pltpu.VMEM((slots + 1, bs, bs), bf16),
             pltpu.VMEM((layouts, own * bs, (col_count + own) * bs), bf16),
             pltpu.VMEM((layouts, own * bs, (col_count + own) * bs), bf16),
             pltpu.SMEM((own, slots), jnp.int32),

time: 61.7 us -> 61.8 us (level)
  no operation moved by 1% of the time
where the time goes in v9:
time: 61.8 us; the launch traced here: 61.6 us
  Pallas kernels  59.8 us (97%)
  local copies, waits for them, and re-layouts  1.77 us (3%)
    pallas_call x1, Pallas kernels, body(): pl.pallas_call(functools.partial(kernel, row_count, col_count), out_shape...  59.8 us
    unnamed x1, local copies, waits for them, and re-layouts  1.77 us

profile of v9, /device:TPU:5, one launch (start us, length us, event | category | flops | bytes accessed | tf_op | source)
XLA Modules:
  0.0 61.6 jit_solution(309873910481242956)
XLA Ops:
  0.0 59.8 %triple_product.1 = f32[64,1536]{1,0:T(8,128)} custom-call(bf16[8,16,128,128]{3,2,1,0:T(8,128)(2,1)} %a_hbm.1, bf16[8,2,128,128]{3,2,1,0:T(8,128)(2,1)} %p_ref.1, s32[8,16]{1,0:T(8,128)} %ac_ref.1, s32[2,8]{1,0:T(2,128)} %bitcast.1, s32[1,24]{1,0:T(1,128)} %sl_ref.1), custom_call_target="tpu_custom_call" | custom-call | tf_op jit(solution)/shard_map/triple_product/pallas_call | solution.py:349
  59.8 1.8 %copy.7 = f32[64,1536]{1,0:T(8,128)} copy(f32[64,1536]{1,0:T(8,128)} %triple_product.1) | data formatting | bytes 786432
